TPU v7x, 32 devices: a whole 2x2x4 slice. The times are simulated.
32 devices in a mesh: blk: 8 (over z, x), mode: 4 (over y, core).
Axes of the slice: x: 2, y: 2, z: 4, core: 2. Of those that a mesh axis runs over, the one named last changes fastest.
Arguments:
- chaos_field: float32 [448, 32768], P('mode', 'blk'), may hold values from -6 to 6
- kl_field: float32 [13, 32768], P(None, 'blk'), may hold values from -1.6 to 4, as said below
- partner: int32 [12, 2, 448], P(None, None, 'mode'), may hold values from 0 to 447, each once within a row
- chaos_coef: float32 [12, 2, 448], P(None, None, 'mode'), may hold values from 0.5 to 2
- cell_count: int32 [8], P('blk'), may hold values from 2048 to 4096, as said below
- face_count: int32 [8, 4], P('blk'), may hold values from 0 to 128, as said below
- face_cells: int32 [8, 4, 128], P('blk'), may hold values from 0 to 4095, as said below
Outputs:
- applied: float32 [448, 32768], P('mode', 'blk')
Inputs may be any that keep to these rules, and one draw needn't show every extreme that they name: A block's live cells are its first cell_count cells, a whole number of rows of 128; some block is full. `face_count`: slots are the neighbouring blocks at offsets -2, -1, +1, +2 of the block index; a pair of blocks has the same count seen from either side, and 0 where the neighbour does not exist. `face_cells`: entry f of a slot pairs with entry f of the neighbour's opposite slot; entries below the count name live cells. `kl_field`: row 0 lies in 0.5 to 4.
All inputs are finite; a program needn't handle non-finite values.
Results may differ from a plain program's by a relative error of at most 0.000068.
Values sent between devices are 32-bit elements; how exact they have to be, the bound alone decides.
A program may use at most 64 MiB of HBM per device.

v0:
```python
import jax
import jax.numpy as jnp
from jax import lax
from jax.sharding import PartitionSpec as P

GZ = 128


SLOT_OFFSETS = (-2, -1, 1, 2)
HIGHEST = lax.Precision.HIGHEST


def shifted(value, axis, steps):
    count = lax.axis_size(axis)
    first, last = (max(0, -steps), min(count, count - steps))
    return lax.ppermute(value, axis, [(source, source + steps) for source in range(first, last)])


def grid_terms(values, conduct, alive_grid):
    down_coef = (
        0.5
        * (conduct[..., 1:, :] + conduct[..., :-1, :])
        * (alive_grid[..., 1:, :] * alive_grid[..., :-1, :])
    )
    down_step = down_coef * (values[..., :-1, :] - values[..., 1:, :])
    side_coef = (
        0.5
        * (conduct[..., :, 1:] + conduct[..., :, :-1])
        * (alive_grid[..., :, 1:] * alive_grid[..., :, :-1])
    )
    side_step = side_coef * (values[..., :, :-1] - values[..., :, 1:])
    leading = [(0, 0)] * (values.ndim - 2)
    result = jnp.pad(down_step, leading + [(0, 1), (0, 0)]) - jnp.pad(
        down_step, leading + [(1, 0), (0, 0)]
    )
    return (
        result
        + jnp.pad(side_step, leading + [(0, 0), (0, 1)])
        - jnp.pad(side_step, leading + [(0, 0), (1, 0)])
    )


def operator_terms(values, conduct, alive_grid, own_flat, face_coef, cells_here):
    modes_here = values.shape[0]
    inside = values[:, :cells_here]
    grid_values = inside.reshape(modes_here, alive_grid.shape[0], alive_grid.shape[1])
    grid_part = grid_terms(grid_values, conduct.reshape(alive_grid.shape), alive_grid).reshape(
        modes_here, cells_here
    )
    own_values = jnp.take(inside, own_flat, axis=1)
    face_part = face_coef[None, :] * (own_values - values[:, cells_here:])
    return (grid_part, face_part)


def neighbour_faces(outgoing):
    pieces = []
    for slot_index, offset in enumerate(SLOT_OFFSETS):
        pieces.append(shifted(outgoing[:, 3 - slot_index], "blk", -offset))
    return jnp.stack(pieces, axis=1)


def per_device(chaos_field, kl_field, partner, chaos_coef, cell_count, face_count, face_cells):
    modes_here, cells_here = chaos_field.shape
    rows_grid = cells_here // GZ
    alive_flag = (lax.iota(jnp.int32, cells_here) < cell_count[0]).astype(jnp.float32)
    alive_grid = alive_flag.reshape(rows_grid, GZ)
    masked = chaos_field * alive_flag[None, :]
    face_limit = face_cells.shape[2]
    own_flat = face_cells[0].reshape(-1)
    face_alive = (
        (lax.iota(jnp.int32, face_limit)[None, :] < face_count[0][:, None])
        .astype(jnp.float32)
        .reshape(-1)
    )
    own_conduct = jnp.take(kl_field, own_flat, axis=1)
    outgoing = jnp.concatenate([jnp.take(masked, own_flat, axis=1), own_conduct], axis=0)
    outgoing = outgoing.reshape(outgoing.shape[0], 4, face_limit)
    arrived = neighbour_faces(outgoing)
    arrived = arrived.reshape(arrived.shape[0], 4 * face_limit)
    remote_field = arrived[:modes_here]
    remote_conduct = arrived[modes_here:]
    face_coefs = 0.5 * (own_conduct + remote_conduct) * face_alive[None, :]
    extended = jnp.concatenate([masked, remote_field], axis=1)
    all_modes = modes_here * lax.axis_size("mode")
    mode_ids = lax.iota(jnp.int32, all_modes)
    mixing_rows = jnp.sum(
        jnp.where(partner[:, :, :, None] == mode_ids, chaos_coef[:, :, :, None], 0.0), axis=1
    )
    random_terms = mixing_rows.shape[0]
    grid_zero, face_zero = operator_terms(
        extended, kl_field[0], alive_grid, own_flat, face_coefs[0], cells_here
    )
    own_term = grid_zero.at[:, own_flat].add(face_zero)
    starting = (
        jnp.zeros((modes_here, cells_here), jnp.float32),
        jnp.zeros((modes_here, 4 * face_limit), jnp.float32),
    )
    portion = lax.all_gather(extended, "mode", axis=0, tiled=True)

    def one_term(kl_index, partial_value):
        mixed_part = jnp.dot(
            mixing_rows[kl_index], portion, precision=HIGHEST, preferred_element_type=jnp.float32
        )
        grid_part, face_part = operator_terms(
            mixed_part,
            kl_field[kl_index + 1],
            alive_grid,
            own_flat,
            face_coefs[kl_index + 1],
            cells_here,
        )
        return (partial_value[0] + grid_part, partial_value[1] + face_part)

    grid_sum, face_sum = lax.fori_loop(0, random_terms, one_term, starting)
    summed = grid_sum.at[:, own_flat].add(face_sum) + own_term
    return summed * alive_flag[None, :]


def solution(mesh):
    in_specs = (
        P("mode", "blk"),
        P(None, "blk"),
        P(None, None, "mode"),
        P(None, None, "mode"),
        P("blk"),
        P("blk", None),
        P("blk", None, None),
    )
    out_specs = P("mode", "blk")
    return jax.shard_map(
        per_device, mesh=mesh, in_specs=in_specs, out_specs=out_specs, check_vma=False
    )
```

profile of v0, /device:TPU:0, one launch (start us, length us, event | category | flops | bytes accessed | tf_op | source)
XLA Modules:
  0.0 398.1 jit_solution(5419778876857081579)
XLA Ops:
  21.4 4.9 %collective-permute-start = (f32[125,128]{0,1:T(8,128)S(1)}, f32[125,128]{0,1:T(8,128)S(1)}, u32[]{:S(2)}, u32[]{:S(2)}) collective-permute-start(f32[125,128]{0,1:T(8,128)S(1)} %get-tuple-element.336), channel_id=1, source_target_pairs={{0,8},{4,12},{8,16},{12,20},{16,24},{20,28},{1,9},{5,13},{9,17},{1... | collective-permute-start | bytes 192008 | tf_op jit(solution)/shard_map/ppermute | solution.py:16
  28.9 4.7 %collective-permute-start.1 = (f32[125,128]{0,1:T(8,128)S(1)}, f32[125,128]{0,1:T(8,128)S(1)}, u32[]{:S(2)}, u32[]{:S(2)}) collective-permute-start(f32[125,128]{0,1:T(8,128)S(1)} %get-tuple-element.339), channel_id=1, source_target_pairs={{0,4},{4,8},{8,12},{12,16},{16,20},{20,24},{24,28},{1,5},{5,9},{9,... | collective-permute-start | bytes 192008 | tf_op jit(solution)/shard_map/ppermute | solution.py:16
  49.1 52.6 %all-gather.2.cloned.1.call-done = f32[448,4608]{1,0:T(8,128)} async-done(((f32[112,4608]{1,0:T(8,128)}), f32[448,4608]{1,0:T(8,128)}) %all-gather.2.cloned.1.call-update) | async-done | bytes 8257552 | tf_op jit(solution)/shard_map/all_gather | solution.py:98
  101.7 269.4 %while.18 = (s32[]{:T(128)}, f32[112,4096]{1,0:T(8,128)}, f32[112,512]{1,0:T(8,128)S(1)}, f32[13,4096]{1,0:T(8,128)}, f32[31,128]{1,0:T(8,128)S(1)}, /*index=5*/...) while((s32[]{:T(128)}, f32[112,4096]{1,0:T(8,128)}, ...), condition=%wide.region_2.4_spmd.clone, body=%wide.region_1.3_spmd.clone.sunk | while | flops 2778941440 | bytes 47211604 | solution.py:114
  103.9 6.7 %fusion.34 = f32[112,4608]{1,0:T(8,128)S(1)} fusion(f32[448,4608]{1,0:T(8,128)} %get-tuple-element.439, f32[12,112,448]{2,1,0:T(8,128)} %get-tuple-element.438, s32[]{:T(128)S(6)} %copy.58), kind=kOutput, calls=%fused_computation.13.clone.1 | convolution fusion | flops 2774532096 | bytes 10551300 | tf_op jit(solution)/shard_map/while/body/eval_jaxpr/dot_general | solution.py:101
  125.0 6.7 %fusion.34 = f32[112,4608]{1,0:T(8,128)S(1)} fusion(f32[448,4608]{1,0:T(8,128)} %get-tuple-element.439, f32[12,112,448]{2,1,0:T(8,128)} %get-tuple-element.438, s32[]{:T(128)S(6)} %copy.58), kind=kOutput, calls=%fused_computation.13.clone.1 | convolution fusion | flops 2774532096 | bytes 10551300 | tf_op jit(solution)/shard_map/while/body/eval_jaxpr/dot_general | solution.py:101
  135.3 4.3 %bitcast_add_fusion.4 = f32[112,4096]{1,0:T(8,128)} fusion(f32[14,8,32,128]{3,2,1,0:T(8,128)S(1)} %bitcast.86, f32[112,4096]{1,0:T(8,128)} %get-tuple-element.420, pred[]{:T(512)S(6)} %compare.11), kind=kLoop, calls=%fused_computation.4.clone.1 | loop fusion | flops 917504 | bytes 5505025 | tf_op jit(solution)/shard_map/while/body/eval_jaxpr/add | solution.py:112
  147.5 6.7 %fusion.34 = f32[112,4608]{1,0:T(8,128)S(1)} fusion(f32[448,4608]{1,0:T(8,128)} %get-tuple-element.439, f32[12,112,448]{2,1,0:T(8,128)} %get-tuple-element.438, s32[]{:T(128)S(6)} %copy.58), kind=kOutput, calls=%fused_computation.13.clone.1 | convolution fusion | flops 2774532096 | bytes 10551300 | tf_op jit(solution)/shard_map/while/body/eval_jaxpr/dot_general | solution.py:101
  157.8 4.3 %bitcast_add_fusion.4 = f32[112,4096]{1,0:T(8,128)} fusion(f32[14,8,32,128]{3,2,1,0:T(8,128)S(1)} %bitcast.86, f32[112,4096]{1,0:T(8,128)} %get-tuple-element.420, pred[]{:T(512)S(6)} %compare.11), kind=kLoop, calls=%fused_computation.4.clone.1 | loop fusion | flops 917504 | bytes 5505025 | tf_op jit(solution)/shard_map/while/body/eval_jaxpr/add | solution.py:112
  170.1 6.7 %fusion.34 = f32[112,4608]{1,0:T(8,128)S(1)} fusion(f32[448,4608]{1,0:T(8,128)} %get-tuple-element.439, f32[12,112,448]{2,1,0:T(8,128)} %get-tuple-element.438, s32[]{:T(128)S(6)} %copy.58), kind=kOutput, calls=%fused_computation.13.clone.1 | convolution fusion | flops 2774532096 | bytes 10551300 | tf_op jit(solution)/shard_map/while/body/eval_jaxpr/dot_general | solution.py:101
  180.4 4.3 %bitcast_add_fusion.4 = f32[112,4096]{1,0:T(8,128)} fusion(f32[14,8,32,128]{3,2,1,0:T(8,128)S(1)} %bitcast.86, f32[112,4096]{1,0:T(8,128)} %get-tuple-element.420, pred[]{:T(512)S(6)} %compare.11), kind=kLoop, calls=%fused_computation.4.clone.1 | loop fusion | flops 917504 | bytes 5505025 | tf_op jit(solution)/shard_map/while/body/eval_jaxpr/add | solution.py:112
  192.7 6.7 %fusion.34 = f32[112,4608]{1,0:T(8,128)S(1)} fusion(f32[448,4608]{1,0:T(8,128)} %get-tuple-element.439, f32[12,112,448]{2,1,0:T(8,128)} %get-tuple-element.438, s32[]{:T(128)S(6)} %copy.58), kind=kOutput, calls=%fused_computation.13.clone.1 | convolution fusion | flops 2774532096 | bytes 10551300 | tf_op jit(solution)/shard_map/while/body/eval_jaxpr/dot_general | solution.py:101
  215.3 6.7 %fusion.34 = f32[112,4608]{1,0:T(8,128)S(1)} fusion(f32[448,4608]{1,0:T(8,128)} %get-tuple-element.439, f32[12,112,448]{2,1,0:T(8,128)} %get-tuple-element.438, s32[]{:T(128)S(6)} %copy.58), kind=kOutput, calls=%fused_computation.13.clone.1 | convolution fusion | flops 2774532096 | bytes 10551300 | tf_op jit(solution)/shard_map/while/body/eval_jaxpr/dot_general | solution.py:101
  237.8 6.7 %fusion.34 = f32[112,4608]{1,0:T(8,128)S(1)} fusion(f32[448,4608]{1,0:T(8,128)} %get-tuple-element.439, f32[12,112,448]{2,1,0:T(8,128)} %get-tuple-element.438, s32[]{:T(128)S(6)} %copy.58), kind=kOutput, calls=%fused_computation.13.clone.1 | convolution fusion | flops 2774532096 | bytes 10551300 | tf_op jit(solution)/shard_map/while/body/eval_jaxpr/dot_general | solution.py:101
  260.4 6.7 %fusion.34 = f32[112,4608]{1,0:T(8,128)S(1)} fusion(f32[448,4608]{1,0:T(8,128)} %get-tuple-element.439, f32[12,112,448]{2,1,0:T(8,128)} %get-tuple-element.438, s32[]{:T(128)S(6)} %copy.58), kind=kOutput, calls=%fused_computation.13.clone.1 | convolution fusion | flops 2774532096 | bytes 10551300 | tf_op jit(solution)/shard_map/while/body/eval_jaxpr/dot_general | solution.py:101
  270.7 4.3 %bitcast_add_fusion.4 = f32[112,4096]{1,0:T(8,128)} fusion(f32[14,8,32,128]{3,2,1,0:T(8,128)S(1)} %bitcast.86, f32[112,4096]{1,0:T(8,128)} %get-tuple-element.420, pred[]{:T(512)S(6)} %compare.11), kind=kLoop, calls=%fused_computation.4.clone.1 | loop fusion | flops 917504 | bytes 5505025 | tf_op jit(solution)/shard_map/while/body/eval_jaxpr/add | solution.py:112
  283.0 6.7 %fusion.34 = f32[112,4608]{1,0:T(8,128)S(1)} fusion(f32[448,4608]{1,0:T(8,128)} %get-tuple-element.439, f32[12,112,448]{2,1,0:T(8,128)} %get-tuple-element.438, s32[]{:T(128)S(6)} %copy.58), kind=kOutput, calls=%fused_computation.13.clone.1 | convolution fusion | flops 2774532096 | bytes 10551300 | tf_op jit(solution)/shard_map/while/body/eval_jaxpr/dot_general | solution.py:101
  293.3 4.3 %bitcast_add_fusion.4 = f32[112,4096]{1,0:T(8,128)} fusion(f32[14,8,32,128]{3,2,1,0:T(8,128)S(1)} %bitcast.86, f32[112,4096]{1,0:T(8,128)} %get-tuple-element.420, pred[]{:T(512)S(6)} %compare.11), kind=kLoop, calls=%fused_computation.4.clone.1 | loop fusion | flops 917504 | bytes 5505025 | tf_op jit(solution)/shard_map/while/body/eval_jaxpr/add | solution.py:112
  305.6 6.7 %fusion.34 = f32[112,4608]{1,0:T(8,128)S(1)} fusion(f32[448,4608]{1,0:T(8,128)} %get-tuple-element.439, f32[12,112,448]{2,1,0:T(8,128)} %get-tuple-element.438, s32[]{:T(128)S(6)} %copy.58), kind=kOutput, calls=%fused_computation.13.clone.1 | convolution fusion | flops 2774532096 | bytes 10551300 | tf_op jit(solution)/shard_map/while/body/eval_jaxpr/dot_general | solution.py:101
  315.9 4.3 %bitcast_add_fusion.4 = f32[112,4096]{1,0:T(8,128)} fusion(f32[14,8,32,128]{3,2,1,0:T(8,128)S(1)} %bitcast.86, f32[112,4096]{1,0:T(8,128)} %get-tuple-element.420, pred[]{:T(512)S(6)} %compare.11), kind=kLoop, calls=%fused_computation.4.clone.1 | loop fusion | flops 917504 | bytes 5505025 | tf_op jit(solution)/shard_map/while/body/eval_jaxpr/add | solution.py:112
  328.1 6.7 %fusion.34 = f32[112,4608]{1,0:T(8,128)S(1)} fusion(f32[448,4608]{1,0:T(8,128)} %get-tuple-element.439, f32[12,112,448]{2,1,0:T(8,128)} %get-tuple-element.438, s32[]{:T(128)S(6)} %copy.58), kind=kOutput, calls=%fused_computation.13.clone.1 | convolution fusion | flops 2774532096 | bytes 10551300 | tf_op jit(solution)/shard_map/while/body/eval_jaxpr/dot_general | solution.py:101
  338.4 4.3 %bitcast_add_fusion.4 = f32[112,4096]{1,0:T(8,128)} fusion(f32[14,8,32,128]{3,2,1,0:T(8,128)S(1)} %bitcast.86, f32[112,4096]{1,0:T(8,128)} %get-tuple-element.420, pred[]{:T(512)S(6)} %compare.11), kind=kLoop, calls=%fused_computation.4.clone.1 | loop fusion | flops 917504 | bytes 5505025 | tf_op jit(solution)/shard_map/while/body/eval_jaxpr/add | solution.py:112
  350.7 6.7 %fusion.34 = f32[112,4608]{1,0:T(8,128)S(1)} fusion(f32[448,4608]{1,0:T(8,128)} %get-tuple-element.439, f32[12,112,448]{2,1,0:T(8,128)} %get-tuple-element.438, s32[]{:T(128)S(6)} %copy.58), kind=kOutput, calls=%fused_computation.13.clone.1 | convolution fusion | flops 2774532096 | bytes 10551300 | tf_op jit(solution)/shard_map/while/body/eval_jaxpr/dot_general | solution.py:101
  377.3 9.9 %scatter_custom_fusion = f32[112,4096]{0,1:T(8,128)} fusion(f32[112,4096]{0,1:T(8,128)} %bitcast_add_fusion.1, s32[1024]{0:T(1024)S(1)} %bitcast.102, f32[112,512]{0,1:T(8,128)S(1)} %subtract_multiply_fusion, f32[]{:T(128)} %constant.120, f32[112,512]{0,1:T(8,128)S(1)} %copy.42), kind=kCustom, calls=%fused_computation.42 | custom fusion | flops 229376 | bytes 2359808 | tf_op jit(solution)/shard_map/add | solution.py:115
  (268 shorter events, 199.0 us)
Async XLA Ops:
  6.5 95.2 %all-gather.2.cloned.1.call-start = ((), (), s32[]{:S(2)}) async-start(), calls=%async_computation | async-start | bytes 10321920 | tf_op jit(solution)/shard_map/all_gather | solution.py:98
  21.4 12.3 %collective-permute-start = (f32[125,128]{0,1:T(8,128)S(1)}, f32[125,128]{0,1:T(8,128)S(1)}, u32[]{:S(2)}, u32[]{:S(2)}) collective-permute-start(f32[125,128]{0,1:T(8,128)S(1)} %get-tuple-element.336), channel_id=1, source_target_pairs={{0,8},{4,12},{8,16},{12,20},{16,24},{20,28},{1,9},{5,13},{9,17},{1... | collective-permute-start | bytes 192008 | tf_op jit(solution)/shard_map/ppermute | solution.py:16
  26.3 7.4 %collective-permute-start.3 = (f32[125,128]{0,1:T(8,128)S(1)}, f32[125,128]{0,1:T(8,128)S(1)}, u32[]{:S(2)}, u32[]{:S(2)}) collective-permute-start(f32[125,128]{0,1:T(8,128)S(1)} %get-tuple-element.337), channel_id=1, source_target_pairs={{8,0},{12,4},{16,8},{20,12},{24,16},{28,20},{9,1},{13,5},{17,9},{2... | collective-permute-start | bytes 192008 | tf_op jit(solution)/shard_map/ppermute | solution.py:16
  27.6 6.2 %collective-permute-start.2 = (f32[125,128]{0,1:T(8,128)S(1)}, f32[125,128]{0,1:T(8,128)S(1)}, u32[]{:S(2)}, u32[]{:S(2)}) collective-permute-start(f32[125,128]{0,1:T(8,128)S(1)} %get-tuple-element.338), channel_id=1, source_target_pairs={{4,0},{8,4},{12,8},{16,12},{20,16},{24,20},{28,24},{5,1},{9,5},{13... | collective-permute-start | bytes 192008 | tf_op jit(solution)/shard_map/ppermute | solution.py:16
  28.9 6.4 %collective-permute-start.1 = (f32[125,128]{0,1:T(8,128)S(1)}, f32[125,128]{0,1:T(8,128)S(1)}, u32[]{:S(2)}, u32[]{:S(2)}) collective-permute-start(f32[125,128]{0,1:T(8,128)S(1)} %get-tuple-element.339), channel_id=1, source_target_pairs={{0,4},{4,8},{8,12},{12,16},{16,20},{20,24},{24,28},{1,5},{5,9},{9,... | collective-permute-start | bytes 192008 | tf_op jit(solution)/shard_map/ppermute | solution.py:16
  43.5 1.9 copy-start.4
  43.5 2.0 copy-start.2
  43.5 2.0 copy-start.3
  45.5 56.2 %copy-start.1 = (s32[1,4,128]{2,1,0:T(4,128)S(1)}, s32[1,4,128]{2,1,0:T(4,128)}, u32[]{:S(2)}) copy-start(s32[1,4,128]{2,1,0:T(4,128)} %param.17) | copy-start | bytes 6148
  371.1 3.2 copy-start
Sparse Core Ops, SparseCore 0:
  40.1 61.5 all-gather.1
where the time goes:
time: 400 us; the launch traced here: 398 us
  local copies, waits for them, and re-layouts  118 us (30%)
  other arithmetic  117 us (29%)
  matrix products  80.7 us (20%)
  waiting for transfers between devices  54.3 us (14%)
  between operations  14.3 us (4%)
  starting transfers between devices  12.3 us (3%)
    dot_general x12, matrix products, one_term(): jnp.dot(mixing_rows[kl_index], portion, precision=HIGHEST, preferred_elem...  80.7 us
    all_gather x1, waiting for transfers between devices, per_device(): portion = lax.all_gather(extended, 'mode', axis=0, tiled=True)  52.6 us
    add x24, other arithmetic, one_term(): return (partial_value[0] + grid_part, partial_value[1] + face_part)  51.9 us
    slice x24, local copies, waits for them, and re-layouts, operator_terms(): inside = values[:, :cells_here]  51.7 us
    gather x24, local copies, waits for them, and re-layouts, operator_terms(): own_values = jnp.take(inside, own_flat, axis=1)  32.9 us
    mul x26, other arithmetic, grid_terms(): 0.5 * (conduct[..., 1:, :] + conduct[..., :-1, :])  14.3 us
    ppermute x4, starting transfers between devices, shifted(): lax.ppermute(value, axis, [(source, source + steps) for source in range(f...  12.3 us
    sub x13, other arithmetic, grid_terms(): result + jnp.pad(side_step, leading + [(0, 0), (0, 1)])  11.6 us
  transfers between devices with their start and end apart: 5, of which 3 were waited for; matrix products, arithmetic and copies ran while one was open for 2% of the time, Pallas kernels for 0%

commit v1 on v0

v1 whole, which is shorter than its diff:
```python
import functools

import jax
import jax.numpy as jnp
from jax import lax
from jax.experimental import pallas as pl
from jax.experimental.pallas import tpu as pltpu
from jax.sharding import PartitionSpec as P

GZ = 128
ROWS = 8
CHUNK = ROWS * GZ
WIDE = 256
TOGETHER = 4
SLOT_OFFSETS = (-2, -1, 1, 2)
VMEM = pl.BlockSpec(memory_space=pltpu.VMEM)
SMEM = pl.BlockSpec(memory_space=pltpu.SMEM)


def params():
    return pltpu.CompilerParams(vmem_limit_bytes=32 * 1024 * 1024)


def cost(flops, size):
    return pl.CostEstimate(flops=flops, bytes_accessed=size, transcendentals=0)


def shifted(value, axis, steps):
    count = lax.axis_size(axis)
    first, last = (max(0, -steps), min(count, count - steps))
    return lax.ppermute(value, axis, [(source, source + steps) for source in range(first, last)])


def split_rows(value):
    high = value.astype(jnp.bfloat16)
    rest = value - high.astype(jnp.float32)
    middle = rest.astype(jnp.bfloat16)
    low = (rest - middle.astype(jnp.float32)).astype(jnp.bfloat16)
    return jnp.concatenate([high, middle, low], axis=0)


def joined(stacked, count):
    return stacked[:count] + (stacked[count : 2 * count] + stacked[2 * count :])


def one_hot(cells, first):
    ids = lax.broadcasted_iota(jnp.int32, (WIDE, cells.shape[1]), 0) + first
    return jnp.where(ids == cells, 1.0, 0.0).astype(jnp.bfloat16)


def gather_kernel(cells_ref, field_ref, out_ref):
    count, width = field_ref.shape
    cells = cells_ref[...]

    def step(at, total):
        first = pl.multiple_of(at * WIDE, WIDE)
        stacked = split_rows(field_ref[:, pl.ds(first, WIDE)])
        return total + jnp.dot(stacked, one_hot(cells, first), preferred_element_type=jnp.float32)

    total = lax.fori_loop(
        0, width // WIDE, step, jnp.zeros((3 * count, cells.shape[1]), jnp.float32)
    )
    out_ref[...] = joined(total, count)


def scatter_kernel(cells_ref, flux_ref, out_ref):
    modes, width = out_ref.shape
    count = flux_ref.shape[0]
    cells = cells_ref[...]
    stacked = split_rows(flux_ref[...])

    @pl.loop(0, width // WIDE)
    def _(at):
        first = pl.multiple_of(at * WIDE, WIDE)
        spread = lax.dot_general(
            stacked,
            one_hot(cells, first),
            (((1,), (1,)), ((), ())),
            preferred_element_type=jnp.float32,
        )
        out_ref[:, pl.ds(first, WIDE)] = joined(spread, count)[:modes]


def group_of(modes):
    return 8 if modes % 8 == 0 else 4


def mix_kernel(modes, slots, random_terms, with_before, with_faces, previous, *refs):
    refs = list(refs)
    take = lambda count: [refs.pop(0) for _ in range(count)]
    partner_ref, weight_ref, coef_ref = take(3)
    parts = take(slots)
    before_ref = take(1)[0] if with_before else None
    face_coef_ref = take(1)[0] if with_faces else None
    face_parts = take(slots) if with_faces else []
    if previous:
        done = take(previous)
        uppers = take(previous)
        face_ref, alive_ref = take(2)
    out_ref, = take(1)
    if not previous:
        upper_ref, lower_ref = take(2)
    flux_ref = take(1)[0] if with_faces else None
    held, result, upper_own, lower_own = take(4)
    if with_faces:
        face_held, face_result = take(2)
    group = group_of(modes)

    for part_list, target, count in ((parts, held, ROWS), (face_parts, face_held if with_faces else None, 4)):
        for slot, part in enumerate(part_list):
            for first in range(0, modes, group):
                for row in range(count):
                    target[pl.ds((slot * modes + first) * ROWS + row, group, stride=ROWS), :] = part[
                        first : first + group, row * GZ : (row + 1) * GZ
                    ]

    row_ids = lax.broadcasted_iota(jnp.int32, (ROWS, GZ), 0)

    @pl.loop(0, modes // TOGETHER)
    def _(turn):
        sums = [[None] * 5 for _ in range(TOGETHER)]

        def add(at, which, value):
            old = sums[at][which]
            sums[at][which] = value if old is None else old + value

        for term in range(random_terms + 1):
            coefs = [coef_ref[which, term] for which in range(4)]
            face_coef = face_coef_ref[term] if with_faces else None
            for at in range(TOGETHER):
                mode = turn * TOGETHER + at
                if term == 0:
                    own = pl.multiple_of(mode * ROWS, ROWS)
                    mixed = held[pl.ds(own, ROWS), :]
                    if with_faces:
                        face_mixed = face_held[pl.ds(own, 4), :]
                else:
                    base = 2 * (term - 1)
                    one = pl.multiple_of(partner_ref[base, mode], ROWS)
                    two = pl.multiple_of(partner_ref[base + 1, mode], ROWS)
                    weight_one = weight_ref[base, mode]
                    weight_two = weight_ref[base + 1, mode]
                    mixed = weight_one * held[pl.ds(one, ROWS), :] + weight_two * held[pl.ds(two, ROWS), :]
                    if with_faces:
                        face_mixed = (
                            weight_one * face_held[pl.ds(one, 4), :]
                            + weight_two * face_held[pl.ds(two, 4), :]
                        )
                for which in range(4):
                    add(at, which, coefs[which] * mixed)
                if with_faces:
                    add(at, 4, face_coef * face_mixed)
        for at in range(TOGETHER):
            mode = turn * TOGETHER + at
            own = pl.multiple_of(mode * ROWS, ROWS)
            down, up, right, left, faces = sums[at]
            from_below = jnp.where(row_ids == ROWS - 1, 0.0, pltpu.roll(up, ROWS - 1, 0))
            from_above = jnp.where(row_ids == 0, 0.0, pltpu.roll(down, 1, 0))
            sideways = pltpu.roll(left, GZ - 1, 1) + pltpu.roll(right, 1, 1)
            result[pl.ds(own, ROWS), :] = (
                (down - from_below) + (up - from_above) + ((right + left) - sideways)
            )
            upper_own[pl.ds(mode, 1), :] = up[0:1]
            lower_own[pl.ds(mode, 1), :] = down[ROWS - 1 : ROWS]
            if with_faces:
                face_result[pl.ds(own, 4), :] = faces

    if with_faces:
        if flux_ref.shape[0] > modes:
            flux_ref[...] = jnp.zeros_like(flux_ref)
        for first in range(0, modes, group):
            for row in range(4):
                flux_ref[first : first + group, row * GZ : (row + 1) * GZ] = face_result[
                    pl.ds(first * ROWS + row, group, stride=ROWS), :
                ]
    offset = previous * CHUNK
    for first in range(0, modes, group):
        some = slice(first, first + group)
        for row in range(ROWS):
            value = result[pl.ds(first * ROWS + row, group, stride=ROWS), :]
            if row == 0 and with_before:
                value = value - before_ref[some, :]
            columns = slice(offset + row * GZ, offset + (row + 1) * GZ)
            if previous:
                value = (value + face_ref[some, columns]) * alive_ref[:, columns]
            out_ref[some, columns] = value
        if previous:
            for at in range(previous):
                for row in range(ROWS):
                    columns = slice(at * CHUNK + row * GZ, at * CHUNK + (row + 1) * GZ)
                    value = done[at][some, row * GZ : (row + 1) * GZ]
                    if row == ROWS - 1:
                        after = uppers[at + 1] if at + 1 < previous else upper_own
                        value = value - after[some, :]
                    out_ref[some, columns] = (value + face_ref[some, columns]) * alive_ref[:, columns]
    if not previous:
        upper_ref[...] = upper_own[...]
        lower_ref[...] = lower_own[...]


def spread_modes(value):
    count = lax.axis_size("mode")
    chips = count // 2
    sibling = [(source, source ^ 1) for source in range(count)]
    pieces = []
    for step in range(chips):
        if step == 0:
            direct = value
        else:
            direct = lax.ppermute(
                value,
                "mode",
                [((target + 2 * step) % count, target) for target in range(count)],
            )
        pieces.append(direct)
        pieces.append(lax.ppermute(direct, "mode", sibling))
    return pieces


def per_device(chaos_field, kl_field, partner, chaos_coef, cell_count, face_count, face_cells):
    modes, cells = chaos_field.shape
    rows_grid = cells // GZ
    chunks = cells // CHUNK
    random_terms = partner.shape[0]
    slots = lax.axis_size("mode")
    face_limit = face_cells.shape[2]
    faces = 4 * face_limit

    raw = [chaos_field[:, at * CHUNK : (at + 1) * CHUNK] for at in range(chunks)]
    gathered = [spread_modes(raw[0]), spread_modes(raw[1])]

    cells_flat = face_cells.reshape(1, faces)
    tall = modes + random_terms + 1
    padded = -(-tall // 16) * 16
    together = jnp.concatenate(
        [chaos_field, kl_field, jnp.zeros((padded - tall, cells), jnp.float32)], axis=0
    )
    own_values = pl.pallas_call(
        gather_kernel,
        out_shape=jax.ShapeDtypeStruct((padded, faces), jnp.float32),
        in_specs=[VMEM, VMEM],
        out_specs=VMEM,
        compiler_params=params(),
        cost_estimate=cost(4_000_000_000, 4 * padded * cells),
    )(cells_flat, together)
    outgoing = own_values[:tall]
    arrived = jnp.concatenate(
        [
            shifted(
                outgoing[:, (3 - slot) * face_limit : (4 - slot) * face_limit], "blk", -offset
            )
            for slot, offset in enumerate(SLOT_OFFSETS)
        ],
        axis=1,
    )
    face_alive = (
        (lax.iota(jnp.int32, face_limit)[None, :] < face_count[0][:, None])
        .astype(jnp.float32)
        .reshape(1, faces)
    )
    face_coef = 0.5 * (outgoing[modes:] + arrived[modes:]) * face_alive
    face_coef = face_coef.reshape(random_terms + 1, 4, face_limit)
    difference = outgoing[:modes] - arrived[:modes]

    alive_flag = (lax.iota(jnp.int32, cells) < cell_count[0]).astype(jnp.float32)
    alive = alive_flag.reshape(rows_grid, GZ)
    conduct = kl_field.reshape(random_terms + 1, rows_grid, GZ)
    down = 0.5 * (conduct[:, 1:] + conduct[:, :-1]) * (alive[1:] * alive[:-1])
    side = 0.5 * (conduct[:, :, 1:] + conduct[:, :, :-1]) * (alive[:, 1:] * alive[:, :-1])
    coefs = jnp.stack(
        [
            jnp.pad(down, ((0, 0), (0, 1), (0, 0))),
            jnp.pad(down, ((0, 0), (1, 0), (0, 0))),
            jnp.pad(side, ((0, 0), (0, 0), (0, 1))),
            jnp.pad(side, ((0, 0), (0, 0), (1, 0))),
        ]
    )

    me = lax.axis_index("mode")
    owner = partner // modes
    step = lax.rem(owner // 2 - me // 2 + slots // 2, slots // 2)
    slot = 2 * step + ((owner ^ me) & 1)
    places = ((slot * modes + lax.rem(partner, modes)) * ROWS).reshape(2 * random_terms, modes)
    weights = chaos_coef.reshape(2 * random_terms, modes)

    face_at = chunks - 2
    face_gathered = spread_modes(difference)
    padded_modes = -(-modes // 16) * 16
    results, uppers, before, face_add = [], [], None, None
    for at in range(chunks):
        last = at == chunks - 1
        with_faces = at == face_at
        if at >= 2:
            held_back, _ = lax.optimization_barrier((raw[at], gathered[at - 2][-2]))
            if last:
                held_back, _ = lax.optimization_barrier((held_back, difference))
            gathered.append(spread_modes(held_back))
        inputs = [places, weights, coefs[:, :, at * ROWS : (at + 1) * ROWS]] + gathered[at]
        in_specs = [SMEM, SMEM] + [VMEM] * (1 + slots)
        if at:
            inputs.append(before)
        if with_faces:
            inputs += [face_coef] + face_gathered
        if last:
            inputs += results + uppers + [face_add, alive_flag[None, :]]
        in_specs += [VMEM] * (len(inputs) - len(in_specs))
        edge = jax.ShapeDtypeStruct((modes, GZ), jnp.float32)
        if last:
            out_shape = [jax.ShapeDtypeStruct((modes, cells), jnp.float32)]
        else:
            out_shape = [jax.ShapeDtypeStruct((modes, CHUNK), jnp.float32), edge, edge]
        if with_faces:
            out_shape.append(jax.ShapeDtypeStruct((padded_modes, faces), jnp.float32))
        scratch = [
            pltpu.VMEM((slots * modes * ROWS, GZ), jnp.float32),
            pltpu.VMEM((modes * ROWS, GZ), jnp.float32),
            pltpu.VMEM((modes, GZ), jnp.float32),
            pltpu.VMEM((modes, GZ), jnp.float32),
        ]
        if with_faces:
            scratch += scratch[:2]
        outs = pl.pallas_call(
            functools.partial(
                mix_kernel, modes, slots, random_terms, at > 0, with_faces, at if last else 0
            ),
            out_shape=out_shape,
            in_specs=in_specs,
            out_specs=[VMEM] * len(out_shape),
            scratch_shapes=scratch,
            compiler_params=params(),
            cost_estimate=cost(5_000_000_000, 4 * slots * modes * CHUNK),
        )(*inputs)
        if last:
            return outs[0]
        results.append(outs[0])
        uppers.append(outs[1])
        before = outs[2]
        if with_faces:
            face_add = pl.pallas_call(
                scatter_kernel,
                out_shape=jax.ShapeDtypeStruct((modes, cells), jnp.float32),
                in_specs=[VMEM, VMEM],
                out_specs=VMEM,
                compiler_params=params(),
                cost_estimate=cost(4_000_000_000, 4 * modes * cells),
            )(cells_flat, outs[3])


def solution(mesh):
    in_specs = (
        P("mode", "blk"),
        P(None, "blk"),
        P(None, None, "mode"),
        P(None, None, "mode"),
        P("blk"),
        P("blk", None),
        P("blk", None, None),
    )
    return jax.shard_map(
        per_device, mesh=mesh, in_specs=in_specs, out_specs=P("mode", "blk"), check_vma=False
    )
```

time: 400 us -> 93.6 us (0.23)
  other arithmetic: 117 us -> 0.8 us
  local copies, waits for them, and re-layouts: 118 us -> 3.61 us
  matrix products: 80.7 us -> 0 us
  Pallas kernels: 0 us -> 43 us
  waiting for transfers between devices: 54.3 us -> 25.3 us
  between operations: 14.3 us -> 0.94 us
  starting transfers between devices: 12.3 us -> 19.6 us
    dot_general x12 -> x0, matrix products: 80.7 us -> none  [one_term(): jnp.dot(mixing_rows[kl_index], portion, precision=HIGHEST, preferred_elem...]
    add x25 -> x0, other arithmetic: 61.8 us -> none  [the longest x24 51.9 us: one_term(): return (partial_value[0] + grid_part, partial_value[1] + face_part)]
    all_gather x1 -> x0, waiting for transfers between devices: 52.6 us -> none  [per_device(): portion = lax.all_gather(extended, 'mode', axis=0, tiled=True)]
    slice x27 -> x3, local copies, waits for them, and re-layouts: 52.9 us -> 2.44 us  [the longest x1 1.74 us: per_device(): raw = [chaos_field[:, at * CHUNK:(at + 1) * CHUNK] for at in range(chunks)]]
    pallas_call x0 -> x6, Pallas kernels: none -> 43 us  [the longest x4 32.6 us: per_device(): pl.pallas_call(functools.partial(mix_kernel, modes, slots, random_terms,...]
    gather x26 -> x0, local copies, waits for them, and re-layouts: 36.6 us -> none  [the longest x24 32.9 us: operator_terms(): own_values = jnp.take(inside, own_flat, axis=1)]
    mul x70 -> x7, other arithmetic: 33 us -> 0.42 us  [the longest x2 0.19 us: per_device(): 0.5 * (conduct[:, :, 1:] + conduct[:, :, :-1])]
    ppermute x4, waiting for transfers between devices: 1.69 us -> 13.7 us  [shifted(): lax.ppermute(value, axis, [(source, source + steps) for source in range(f...]
  transfers between devices with their start and end apart: 5 -> 19, of which waited for: 3 -> 6; matrix products, arithmetic and copies ran while one was open for 2% -> 2% of each run, Pallas kernels for 0% -> 37%
where the time goes in v1:
time: 93.6 us; the launch traced here: 93.3 us
  Pallas kernels  43 us (46%)
  waiting for transfers between devices  25.3 us (27%)
  starting transfers between devices  19.6 us (21%)
  local copies, waits for them, and re-layouts  3.61 us (4%)
  between operations  0.94 us (1%)
    pallas_call x4, Pallas kernels, per_device(): pl.pallas_call(functools.partial(mix_kernel, modes, slots, random_terms,...  32.6 us
    ppermute x4, waiting for transfers between devices, shifted(): lax.ppermute(value, axis, [(source, source + steps) for source in range(f...  13.7 us
    ppermute x5, waiting for transfers between devices, spread_modes(): lax.ppermute(value, 'mode', [((target + 2 * step) % count, target) for ta...  11.6 us
    ppermute x4, starting transfers between devices, shifted(): lax.ppermute(value, axis, [(source, source + steps) for source in range(f...  9.65 us
    ppermute x5, starting transfers between devices, spread_modes(): lax.ppermute(value, 'mode', [((target + 2 * step) % count, target) for ta...  7.49 us
    pallas_call x1, Pallas kernels, per_device(): pl.pallas_call(gather_kernel, out_shape=jax.ShapeDtypeStruct((padded, fac...  5.74 us
    pallas_call x1, Pallas kernels, per_device(): pl.pallas_call(scatter_kernel, out_shape=jax.ShapeDtypeStruct((modes, cel...  4.71 us
    ppermute x10, starting transfers between devices, spread_modes(): pieces.append(lax.ppermute(direct, 'mode', sibling))  2.41 us
  transfers between devices with their start and end apart: 19, of which 6 were waited for; matrix products, arithmetic and copies ran while one was open for 2% of the time, Pallas kernels for 37%

profile of v1, /device:TPU:0, one launch (start us, length us, event | category | flops | bytes accessed | tf_op | source)
XLA Modules:
  0.0 93.3 jit_solution(10491059336326368541)
XLA Ops:
  0.0 1.7 %fusion.9 = (f32[112,1024]{1,0:T(8,128)S(1)}, f32[112,1024]{1,0:T(8,128)S(1)}, f32[112,1024]{1,0:T(8,128)S(1)}, f32[112,1024]{1,0:T(8,128)S(1)}) fusion(f32[112,4096]{1,0:T(8,128)} %param.7), kind=kLoop, calls=%fused_computation.37 | loop fusion | bytes 3670016 | tf_op jit(solution)/shard_map/slice | solution.py:229
  2.3 2.6 %collective-permute-start.8 = (f32[112,1024]{1,0:T(8,128)S(1)}, f32[112,1024]{1,0:T(8,128)}, u32[]{:S(2)}, u32[]{:S(2)}) collective-permute-start(f32[112,1024]{1,0:T(8,128)S(1)} %get-tuple-element.31.refs_3_), channel_id=1, source_target_pairs={{2,0},{3,1},{0,2},{1,3},{6,4},{7,5},{4,6},{5,7},{10,8},{11,9},{8,1... | collective-permute-start | bytes 1376264 | tf_op jit(solution)/shard_map/ppermute | solution.py:210
  6.1 5.7 %shard_map.73 = f32[128,512]{1,0:T(8,128)S(1)} custom-call(s32[1,512]{1,0:T(1,128)S(1)} %bitcast.28, f32[128,4096]{1,0:T(8,128)S(1)} %maximum_maximum_fusion.field_ref), custom_call_target="tpu_custom_call" | custom-call | flops 4000000000 | bytes 2097152 | tf_op jit(solution)/shard_map/pallas_call | solution.py:238
  11.8 0.6 fusion.11
  12.5 3.7 %collective-permute-start.1 = (f32[125,128]{1,0:T(8,128)S(1)}, f32[125,128]{1,0:T(8,128)S(1)}, u32[]{:S(2)}, u32[]{:S(2)}) collective-permute-start(f32[125,128]{1,0:T(8,128)S(1)} %get-tuple-element.42), channel_id=1, source_target_pairs={{0,8},{4,12},{8,16},{12,20},{16,24},{20,28},{1,9},{5,13},{9,17},{1... | collective-permute-start | bytes 192008 | tf_op jit(solution)/shard_map/ppermute | solution.py:31
  18.1 3.4 %collective-permute-start.2 = (f32[125,128]{1,0:T(8,128)S(1)}, f32[125,128]{1,0:T(8,128)S(1)}, u32[]{:S(2)}, u32[]{:S(2)}) collective-permute-start(f32[125,128]{1,0:T(8,128)S(1)} %get-tuple-element.41), channel_id=1, source_target_pairs={{0,4},{4,8},{8,12},{12,16},{16,20},{20,24},{24,28},{1,5},{5,9},{9,... | collective-permute-start | bytes 192008 | tf_op jit(solution)/shard_map/ppermute | solution.py:31
  21.5 1.9 %collective-permute-done.2 = f32[125,128]{1,0:T(8,128)S(1)} collective-permute-done((f32[125,128]{1,0:T(8,128)S(1)}, f32[125,128]{1,0:T(8,128)S(1)}, u32[]{:S(2)}, u32[]{:S(2)}) %collective-permute-start.2) | collective-permute-done | bytes 64032 | tf_op jit(solution)/shard_map/ppermute | solution.py:31
  23.3 1.3 %collective-permute-start.3 = (f32[125,128]{1,0:T(8,128)S(1)}, f32[125,128]{1,0:T(8,128)S(1)}, u32[]{:S(2)}, u32[]{:S(2)}) collective-permute-start(f32[125,128]{1,0:T(8,128)S(1)} %get-tuple-element.40), channel_id=1, source_target_pairs={{4,0},{8,4},{12,8},{16,12},{20,16},{24,20},{28,24},{5,1},{9,5},{13... | collective-permute-start | bytes 192008 | tf_op jit(solution)/shard_map/ppermute | solution.py:31
  24.6 5.2 %collective-permute-done.3 = f32[125,128]{1,0:T(8,128)S(1)} collective-permute-done((f32[125,128]{1,0:T(8,128)S(1)}, f32[125,128]{1,0:T(8,128)S(1)}, u32[]{:S(2)}, u32[]{:S(2)}) %collective-permute-start.3) | collective-permute-done | bytes 64032 | tf_op jit(solution)/shard_map/ppermute | solution.py:31
  29.8 1.3 %collective-permute-start.4 = (f32[125,128]{1,0:T(8,128)S(1)}, f32[125,128]{1,0:T(8,128)S(1)}, u32[]{:S(2)}, u32[]{:S(2)}) collective-permute-start(f32[125,128]{1,0:T(8,128)S(1)} %copy-done.4), channel_id=1, source_target_pairs={{8,0},{12,4},{16,8},{20,12},{24,16},{28,20},{9,1},{13,5},{17,9},{2... | collective-permute-start | bytes 192008 | tf_op jit(solution)/shard_map/ppermute | solution.py:31
  31.1 6.6 %collective-permute-done.4 = f32[125,128]{1,0:T(8,128)S(1)} collective-permute-done((f32[125,128]{1,0:T(8,128)S(1)}, f32[125,128]{1,0:T(8,128)S(1)}, u32[]{:S(2)}, u32[]{:S(2)}) %collective-permute-start.4) | collective-permute-done | bytes 64032 | tf_op jit(solution)/shard_map/ppermute | solution.py:31
  37.9 1.6 %collective-permute-start.17 = (f32[112,512]{1,0:T(8,128)S(1)}, f32[112,512]{1,0:T(8,128)S(1)}, u32[]{:S(2)}, u32[]{:S(2)}) collective-permute-start(f32[112,512]{1,0:T(8,128)S(1)} %slice_subtract_fusion.refs_9_), channel_id=1, source_target_pairs={{2,0},{3,1},{0,2},{1,3},{6,4},{7,5},{4,6},{5,7},{10,8},{11,9},{8,1... | collective-permute-start | bytes 688136 | tf_op jit(solution)/shard_map/ppermute | solution.py:210
  39.6 6.4 %collective-permute-done.17.refs_11_ = f32[112,512]{1,0:T(8,128)S(1)} collective-permute-done((f32[112,512]{1,0:T(8,128)S(1)}, f32[112,512]{1,0:T(8,128)S(1)}, u32[]{:S(2)}, u32[]{:S(2)}) %collective-permute-start.17) | collective-permute-done | bytes 229408 | tf_op jit(solution)/shard_map/ppermute | solution.py:210
  46.5 1.5 %collective-permute-start.10 = (f32[112,1024]{1,0:T(8,128)S(1)}, f32[112,1024]{1,0:T(8,128)S(1)}, u32[]{:S(2)}, u32[]{:S(2)}) collective-permute-start(f32[112,1024]{1,0:T(8,128)S(1)} %get-tuple-element.20.refs_3_), channel_id=1, source_target_pairs={{2,0},{3,1},{0,2},{1,3},{6,4},{7,5},{4,6},{5,7},{10,8},{11,9},{8,1... | collective-permute-start | bytes 1376264 | tf_op jit(solution)/shard_map/ppermute | solution.py:210
  48.0 7.4 %shard_map.74 = (f32[112,1024]{1,0:T(8,128)S(1)}, f32[112,128]{1,0:T(8,128)S(1)}, f32[112,128]{1,0:T(8,128)S(1)}) custom-call(s32[24,112]{1,0:T(8,128)S(1)} %bitcast.20, f32[24,112]{1,0:T(8,128)S(1)} %bitcast.24, f32[4,13,8,128]{3,2,1,0:T(8,128)S(1)} %get-tuple-element.35.refs_2_, f32[112,1024]{1,0:T(8,128)S(1)} %get-tuple-element.31.refs_3_, ...), custom_call_target="tpu_custom_call" | custom-call | flops 5000000000 | bytes 1835008 | tf_op jit(solution)/shard_map/pallas_call | solution.py:322
  55.5 0.6 collective-permute-start.9
  56.0 2.9 %collective-permute-done.10.refs_5_ = f32[112,1024]{1,0:T(8,128)S(1)} collective-permute-done((f32[112,1024]{1,0:T(8,128)S(1)}, f32[112,1024]{1,0:T(8,128)S(1)}, u32[]{:S(2)}, u32[]{:S(2)}) %collective-permute-start.10) | collective-permute-done | bytes 458784 | tf_op jit(solution)/shard_map/ppermute | solution.py:210
  59.0 1.5 %collective-permute-start.6 = (f32[112,1024]{1,0:T(8,128)S(1)}, f32[112,1024]{1,0:T(8,128)S(1)}, u32[]{:S(2)}, u32[]{:S(2)}) collective-permute-start(f32[112,1024]{1,0:T(8,128)S(1)} %get-tuple-element.19.refs_3_), channel_id=1, source_target_pairs={{2,0},{3,1},{0,2},{1,3},{6,4},{7,5},{4,6},{5,7},{10,8},{11,9},{8,1... | collective-permute-start | bytes 1376264 | tf_op jit(solution)/shard_map/ppermute | solution.py:210
  60.5 7.3 %shard_map.75 = (f32[112,1024]{1,0:T(8,128)S(1)}, f32[112,128]{1,0:T(8,128)S(1)}, f32[112,128]{1,0:T(8,128)S(1)}) custom-call(s32[24,112]{1,0:T(8,128)S(1)} %bitcast.21, f32[24,112]{1,0:T(8,128)S(1)} %bitcast.25, f32[4,13,8,128]{3,2,1,0:T(8,128)S(1)} %get-tuple-element.36.refs_2_, f32[112,1024]{1,0:T(8,128)S(1)} %get-tuple-element.32.refs_3_, ...), custom_call_target="tpu_custom_call" | custom-call | flops 5000000000 | bytes 1835008 | tf_op jit(solution)/shard_map/pallas_call | solution.py:322
  67.8 0.6 collective-permute-start.5
  68.4 2.2 %collective-permute-done.6.refs_5_ = f32[112,1024]{1,0:T(8,128)S(1)} collective-permute-done((f32[112,1024]{1,0:T(8,128)S(1)}, f32[112,1024]{1,0:T(8,128)S(1)}, u32[]{:S(2)}, u32[]{:S(2)}) %collective-permute-start.6) | collective-permute-done | bytes 458784 | tf_op jit(solution)/shard_map/ppermute | solution.py:210
  70.6 9.3 %shard_map.76 = (f32[112,1024]{1,0:T(8,128)S(1)}, f32[112,128]{1,0:T(8,128)S(1)}, f32[112,128]{1,0:T(8,128)S(1)}, f32[112,512]{1,0:T(8,128)S(1)}) custom-call(s32[24,112]{1,0:T(8,128)S(1)} %bitcast.22, f32[24,112]{1,0:T(8,128)S(1)} %bitcast.26, f32[4,13,8,128]{3,2,1,0:T(8,128)S(1)} %get-tuple-element.37.refs_2_, f32[112,1024]{1,0:T(8,128)S(1)} %get-tuple-element.20.refs_3_, ...), custom_call_target="tpu_custom_call" | custom-call | flops 5000000000 | bytes 1835008 | tf_op jit(solution)/shard_map/pallas_call | solution.py:322
  80.0 4.7 %shard_map.77.refs_14_ = f32[112,4096]{1,0:T(8,128)S(1)} custom-call(s32[1,512]{1,0:T(1,128)S(1)} %bitcast.29, f32[112,512]{1,0:T(8,128)S(1)} %get-tuple-element.30.flux_ref), custom_call_target="tpu_custom_call" | custom-call | flops 4000000000 | bytes 1835008 | tf_op jit(solution)/shard_map/pallas_call | solution.py:339
  84.7 8.5 %shard_map.78 = f32[112,4096]{1,0:T(8,128)} custom-call(s32[24,112]{1,0:T(8,128)S(1)} %bitcast.23, f32[24,112]{1,0:T(8,128)S(1)} %bitcast.27, f32[4,13,8,128]{3,2,1,0:T(8,128)S(1)} %get-tuple-element.38.refs_2_, f32[112,1024]{1,0:T(8,128)S(1)} %get-tuple-element.19.refs_3_, f32[112,1024]{1,0:T(8,128)S(1)} %collective-permute-done.5.refs_4_, ...), custom_call_target="tpu_custom_call" | custom-call | flops 5000000000 | bytes 1835008 | tf_op jit(solution)/shard_map/pallas_call | solution.py:322
  (59 shorter events, 3.6 us)
Async XLA Ops:
  0.0 5.4 %copy-start.2 = (f32[112,4096]{1,0:T(8,128)S(1)}, f32[112,4096]{1,0:T(8,128)}, u32[]{:S(2)}) copy-start(f32[112,4096]{1,0:T(8,128)} %param.7) | copy-start | bytes 5505028
  0.0 5.4 %copy-start.3 = (f32[13,4096]{1,0:T(8,128)S(1)}, f32[13,4096]{1,0:T(8,128)}, u32[]{:S(2)}) copy-start(f32[13,4096]{1,0:T(8,128)} %param.8) | copy-start | bytes 638980
  1.8 44.7 %collective-permute-start.14 = (f32[112,1024]{1,0:T(8,128)S(1)}, f32[112,1024]{1,0:T(8,128)}, u32[]{:S(2)}, u32[]{:S(2)}) collective-permute-start(f32[112,1024]{1,0:T(8,128)S(1)} %get-tuple-element.31.refs_3_), channel_id=1, source_target_pairs={{0,1},{1,0},{2,3},{3,2},{4,5},{5,4},{6,7},{7,6},{8,9},{9,8},{10,11... | collective-permute-start | bytes 1376264 | tf_op jit(solution)/shard_map/ppermute | solution.py:216
  2.3 35.5 %collective-permute-start.8 = (f32[112,1024]{1,0:T(8,128)S(1)}, f32[112,1024]{1,0:T(8,128)}, u32[]{:S(2)}, u32[]{:S(2)}) collective-permute-start(f32[112,1024]{1,0:T(8,128)S(1)} %get-tuple-element.31.refs_3_), channel_id=1, source_target_pairs={{2,0},{3,1},{0,2},{1,3},{6,4},{7,5},{4,6},{5,7},{10,8},{11,9},{8,1... | collective-permute-start | bytes 1376264 | tf_op jit(solution)/shard_map/ppermute | solution.py:210
  4.9 50.6 %collective-permute-start.12 = (f32[112,1024]{1,0:T(8,128)S(1)}, f32[112,1024]{1,0:T(8,128)}, u32[]{:S(2)}, u32[]{:S(2)}) collective-permute-start(f32[112,1024]{1,0:T(8,128)S(1)} %get-tuple-element.32.refs_3_), channel_id=1, source_target_pairs={{0,1},{1,0},{2,3},{3,2},{4,5},{5,4},{6,7},{7,6},{8,9},{9,8},{10,11... | collective-permute-start | bytes 1376264 | tf_op jit(solution)/shard_map/ppermute | solution.py:216
  5.0 40.9 %collective-permute-start = (f32[112,1024]{1,0:T(8,128)S(1)}, f32[112,1024]{1,0:T(8,128)}, u32[]{:S(2)}, u32[]{:S(2)}) collective-permute-start(f32[112,1024]{1,0:T(8,128)S(1)} %get-tuple-element.32.refs_3_), channel_id=1, source_target_pairs={{2,0},{3,1},{0,2},{1,3},{6,4},{7,5},{4,6},{5,7},{10,8},{11,9},{8,1... | collective-permute-start | bytes 1376264 | tf_op jit(solution)/shard_map/ppermute | solution.py:210
  12.5 5.6 %collective-permute-start.1 = (f32[125,128]{1,0:T(8,128)S(1)}, f32[125,128]{1,0:T(8,128)S(1)}, u32[]{:S(2)}, u32[]{:S(2)}) collective-permute-start(f32[125,128]{1,0:T(8,128)S(1)} %get-tuple-element.42), channel_id=1, source_target_pairs={{0,8},{4,12},{8,16},{12,20},{16,24},{20,28},{1,9},{5,13},{9,17},{1... | collective-permute-start | bytes 192008 | tf_op jit(solution)/shard_map/ppermute | solution.py:31
  17.4 12.5 %copy-start.4 = (f32[125,128]{1,0:T(8,128)S(1)}, f32[125,128]{1,0:T(8,128)}, u32[]{:S(2)}) copy-start(f32[125,128]{1,0:T(8,128)} %get-tuple-element.39) | copy-start | bytes 192004
  17.4 22.1 %copy-start.6 = (s32[1,4]{1,0:T(1,128)S(1)}, s32[1,4]{1,0:T(1,128)}, u32[]{:S(2)}) copy-start(s32[1,4]{1,0:T(1,128)} %param.12) | copy-start | bytes 52
  17.4 30.6 %copy-start = (f32[12,2,112]{2,1,0:T(2,128)S(1)}, f32[12,2,112]{2,1,0:T(2,128)}, u32[]{:S(2)}) copy-start(f32[12,2,112]{2,1,0:T(2,128)} %param.10) | copy-start | bytes 32260
  18.1 5.3 %collective-permute-start.2 = (f32[125,128]{1,0:T(8,128)S(1)}, f32[125,128]{1,0:T(8,128)S(1)}, u32[]{:S(2)}, u32[]{:S(2)}) collective-permute-start(f32[125,128]{1,0:T(8,128)S(1)} %get-tuple-element.41), channel_id=1, source_target_pairs={{0,4},{4,8},{8,12},{12,16},{16,20},{20,24},{24,28},{1,5},{5,9},{9,... | collective-permute-start | bytes 192008 | tf_op jit(solution)/shard_map/ppermute | solution.py:31
  23.3 6.5 %collective-permute-start.3 = (f32[125,128]{1,0:T(8,128)S(1)}, f32[125,128]{1,0:T(8,128)S(1)}, u32[]{:S(2)}, u32[]{:S(2)}) collective-permute-start(f32[125,128]{1,0:T(8,128)S(1)} %get-tuple-element.40), channel_id=1, source_target_pairs={{4,0},{8,4},{12,8},{16,12},{20,16},{24,20},{28,24},{5,1},{9,5},{13... | collective-permute-start | bytes 192008 | tf_op jit(solution)/shard_map/ppermute | solution.py:31
  29.8 7.9 %collective-permute-start.4 = (f32[125,128]{1,0:T(8,128)S(1)}, f32[125,128]{1,0:T(8,128)S(1)}, u32[]{:S(2)}, u32[]{:S(2)}) collective-permute-start(f32[125,128]{1,0:T(8,128)S(1)} %copy-done.4), channel_id=1, source_target_pairs={{8,0},{12,4},{16,8},{20,12},{24,16},{28,20},{9,1},{13,5},{17,9},{2... | collective-permute-start | bytes 192008 | tf_op jit(solution)/shard_map/ppermute | solution.py:31
  37.8 10.2 %collective-permute-start.15 = (f32[112,1024]{1,0:T(8,128)}, f32[112,1024]{1,0:T(8,128)}, u32[]{:S(2)}, u32[]{:S(2)}) collective-permute-start(f32[112,1024]{1,0:T(8,128)} %collective-permute-done.8.refs_5_), channel_id=1, source_target_pairs={{0,1},{1,0},{2,3},{3,2},{4,5},{5,4},{6,7},{7,6},{8,9},{9,8},{10,11... | collective-permute-start | bytes 1376264 | tf_op jit(solution)/shard_map/ppermute | solution.py:216
  37.9 8.1 %collective-permute-start.17 = (f32[112,512]{1,0:T(8,128)S(1)}, f32[112,512]{1,0:T(8,128)S(1)}, u32[]{:S(2)}, u32[]{:S(2)}) collective-permute-start(f32[112,512]{1,0:T(8,128)S(1)} %slice_subtract_fusion.refs_9_), channel_id=1, source_target_pairs={{2,0},{3,1},{0,2},{1,3},{6,4},{7,5},{4,6},{5,7},{10,8},{11,9},{8,1... | collective-permute-start | bytes 688136 | tf_op jit(solution)/shard_map/ppermute | solution.py:210
  46.0 21.8 %collective-permute-start.16 = (f32[112,512]{1,0:T(8,128)S(1)}, f32[112,512]{1,0:T(8,128)S(1)}, u32[]{:S(2)}, u32[]{:S(2)}) collective-permute-start(f32[112,512]{1,0:T(8,128)S(1)} %slice_subtract_fusion.refs_9_), channel_id=1, source_target_pairs={{0,1},{1,0},{2,3},{3,2},{4,5},{5,4},{6,7},{7,6},{8,9},{9,8},{10,11... | collective-permute-start | bytes 688136 | tf_op jit(solution)/shard_map/ppermute | solution.py:216
  46.0 24.7 %collective-permute-start.18 = (f32[112,512]{1,0:T(8,128)S(1)}, f32[112,512]{1,0:T(8,128)S(1)}, u32[]{:S(2)}, u32[]{:S(2)}) collective-permute-start(f32[112,512]{1,0:T(8,128)S(1)} %collective-permute-done.17.refs_11_), channel_id=1, source_target_pairs={{0,1},{1,0},{2,3},{3,2},{4,5},{5,4},{6,7},{7,6},{8,9},{9,8},{10,11... | collective-permute-start | bytes 688136 | tf_op jit(solution)/shard_map/ppermute | solution.py:216
  46.5 12.5 %collective-permute-start.10 = (f32[112,1024]{1,0:T(8,128)S(1)}, f32[112,1024]{1,0:T(8,128)S(1)}, u32[]{:S(2)}, u32[]{:S(2)}) collective-permute-start(f32[112,1024]{1,0:T(8,128)S(1)} %get-tuple-element.20.refs_3_), channel_id=1, source_target_pairs={{2,0},{3,1},{0,2},{1,3},{6,4},{7,5},{4,6},{5,7},{10,8},{11,9},{8,1... | collective-permute-start | bytes 1376264 | tf_op jit(solution)/shard_map/ppermute | solution.py:210
  48.0 12.5 %collective-permute-start.13 = (f32[112,1024]{1,0:T(8,128)}, f32[112,1024]{1,0:T(8,128)S(1)}, u32[]{:S(2)}, u32[]{:S(2)}) collective-permute-start(f32[112,1024]{1,0:T(8,128)} %collective-permute-done.refs_5_), channel_id=1, source_target_pairs={{0,1},{1,0},{2,3},{3,2},{4,5},{5,4},{6,7},{7,6},{8,9},{9,8},{10,11... | collective-permute-start | bytes 1376264 | tf_op jit(solution)/shard_map/ppermute | solution.py:216
  55.5 15.2 %collective-permute-start.9 = (f32[112,1024]{1,0:T(8,128)S(1)}, f32[112,1024]{1,0:T(8,128)S(1)}, u32[]{:S(2)}, u32[]{:S(2)}) collective-permute-start(f32[112,1024]{1,0:T(8,128)S(1)} %get-tuple-element.20.refs_3_), channel_id=1, source_target_pairs={{0,1},{1,0},{2,3},{3,2},{4,5},{5,4},{6,7},{7,6},{8,9},{9,8},{10,11... | collective-permute-start | bytes 1376264 | tf_op jit(solution)/shard_map/ppermute | solution.py:216
  59.0 11.7 %collective-permute-start.6 = (f32[112,1024]{1,0:T(8,128)S(1)}, f32[112,1024]{1,0:T(8,128)S(1)}, u32[]{:S(2)}, u32[]{:S(2)}) collective-permute-start(f32[112,1024]{1,0:T(8,128)S(1)} %get-tuple-element.19.refs_3_), channel_id=1, source_target_pairs={{2,0},{3,1},{0,2},{1,3},{6,4},{7,5},{4,6},{5,7},{10,8},{11,9},{8,1... | collective-permute-start | bytes 1376264 | tf_op jit(solution)/shard_map/ppermute | solution.py:210
  60.5 10.1 %collective-permute-start.11 = (f32[112,1024]{1,0:T(8,128)S(1)}, f32[112,1024]{1,0:T(8,128)S(1)}, u32[]{:S(2)}, u32[]{:S(2)}) collective-permute-start(f32[112,1024]{1,0:T(8,128)S(1)} %collective-permute-done.10.refs_5_), channel_id=1, source_target_pairs={{0,1},{1,0},{2,3},{3,2},{4,5},{5,4},{6,7},{7,6},{8,9},{9,8},{10,11... | collective-permute-start | bytes 1376264 | tf_op jit(solution)/shard_map/ppermute | solution.py:216
  67.8 16.9 %collective-permute-start.5 = (f32[112,1024]{1,0:T(8,128)S(1)}, f32[112,1024]{1,0:T(8,128)S(1)}, u32[]{:S(2)}, u32[]{:S(2)}) collective-permute-start(f32[112,1024]{1,0:T(8,128)S(1)} %get-tuple-element.19.refs_3_), channel_id=1, source_target_pairs={{0,1},{1,0},{2,3},{3,2},{4,5},{5,4},{6,7},{7,6},{8,9},{9,8},{10,11... | collective-permute-start | bytes 1376264 | tf_op jit(solution)/shard_map/ppermute | solution.py:216
  70.6 14.1 %collective-permute-start.7 = (f32[112,1024]{1,0:T(8,128)S(1)}, f32[112,1024]{1,0:T(8,128)S(1)}, u32[]{:S(2)}, u32[]{:S(2)}) collective-permute-start(f32[112,1024]{1,0:T(8,128)S(1)} %collective-permute-done.6.refs_5_), channel_id=1, source_target_pairs={{0,1},{1,0},{2,3},{3,2},{4,5},{5,4},{6,7},{7,6},{8,9},{9,8},{10,11... | collective-permute-start | bytes 1376264 | tf_op jit(solution)/shard_map/ppermute | solution.py:216
  (2 other events, 1.4 us)

commit v2 on v1

v2 whole, which is shorter than its diff:
```python
import functools

import jax
import jax.numpy as jnp
from jax import lax
from jax.experimental import pallas as pl
from jax.experimental.pallas import tpu as pltpu
from jax.sharding import PartitionSpec as P

GZ = 128
TILE = 8
WIDE = 256
TOGETHER = 4
SLOT_OFFSETS = (-2, -1, 1, 2)
VMEM = pl.BlockSpec(memory_space=pltpu.VMEM)
SMEM = pl.BlockSpec(memory_space=pltpu.SMEM)


def params():
    return pltpu.CompilerParams(vmem_limit_bytes=32 * 1024 * 1024)


def cost(flops, size):
    return pl.CostEstimate(flops=flops, bytes_accessed=size, transcendentals=0)


def split_rows(value):
    high = value.astype(jnp.bfloat16)
    low = (value - high.astype(jnp.float32)).astype(jnp.bfloat16)
    return jnp.concatenate([high, low], axis=0)


def joined(stacked, count):
    return stacked[:count] + stacked[count:]


def one_hot(cells, first):
    ids = lax.broadcasted_iota(jnp.int32, (WIDE, cells.shape[1]), 0) + first
    return jnp.where(ids == cells, 1.0, 0.0).astype(jnp.bfloat16)


def chunk_rows(rows_grid):
    half = rows_grid // 2 // TILE * TILE
    rest = rows_grid - half
    return [half] + [TILE] * (rest // TILE)


def relayout_kernel(sizes, field_ref, *out_refs):
    modes = field_ref.shape[0]
    group = group_of(modes)
    start = 0
    for size, out_ref in zip(sizes, out_refs):
        for first in range(0, modes, group):
            for row in range(size):
                columns = slice((start + row) * GZ, (start + row + 1) * GZ)
                out_ref[pl.ds(first * size + row, group, stride=size), :] = field_ref[
                    first : first + group, columns
                ]
        start += size


def face_kernel(
    count, lead, cells_ref, field_ref, kl_ref, out_ref, conduct_ref, both, own, arrived, send, recv
):
    modes, width = field_ref.shape
    padded = both.shape[0]
    limit = own.shape[2]
    me = lax.axis_index("blk")
    barrier = pltpu.get_barrier_semaphore()
    exists, copies = [], []
    for slot, offset in enumerate(SLOT_OFFSETS):
        there = (me + offset >= 0) & (me + offset < count)
        exists.append(there)
        copies.append(
            pltpu.make_async_remote_copy(
                src_ref=own.at[slot],
                dst_ref=arrived.at[3 - slot],
                send_sem=send.at[slot],
                recv_sem=recv.at[3 - slot],
                device_id={"blk": me + offset},
                device_id_type=pl.DeviceIdType.MESH,
            )
        )

        @pl.when(there)
        def _():
            pl.semaphore_signal(
                barrier,
                inc=1,
                device_id={"blk": me + offset},
                device_id_type=pl.DeviceIdType.MESH,
            )

    both[...] = jnp.zeros_like(both)
    both[: kl_ref.shape[0], :] = kl_ref[...]
    both[lead : lead + modes, :] = field_ref[...]
    cells = cells_ref[...]

    def step(at, total):
        first = pl.multiple_of(at * WIDE, WIDE)
        stacked = split_rows(both[:, pl.ds(first, WIDE)])
        return total + jnp.dot(stacked, one_hot(cells, first), preferred_element_type=jnp.float32)

    total = lax.fori_loop(
        0, width // WIDE, step, jnp.zeros((2 * padded, cells.shape[1]), jnp.float32)
    )
    values = joined(total, padded)
    for slot in range(4):
        own[slot] = values[:, slot * limit : (slot + 1) * limit]

    pl.semaphore_wait(barrier, sum(there.astype(jnp.int32) for there in exists))

    for slot in range(4):
        @pl.when(exists[slot])
        def _():
            copies[slot].start()

        @pl.when(jnp.logical_not(exists[slot]))
        def _():
            arrived[slot] = jnp.zeros_like(arrived[slot])

    for slot in range(4):
        @pl.when(exists[slot])
        def _():
            copies[slot].wait_send()
            pltpu.make_async_remote_copy(
                src_ref=own.at[slot],
                dst_ref=arrived.at[slot],
                send_sem=send.at[slot],
                recv_sem=recv.at[slot],
                device_id={"blk": me + SLOT_OFFSETS[slot]},
                device_id_type=pl.DeviceIdType.MESH,
            ).wait_recv()

    for slot in range(4):
        out_ref[:, slot * limit : (slot + 1) * limit] = (
            own[slot, lead : lead + modes, :] - arrived[slot, lead : lead + modes, :]
        )
        conduct_ref[slot] = own[slot, :lead, :] + arrived[slot, :lead, :]


def scatter_kernel(cells_ref, flux_ref, out_ref):
    modes, width = out_ref.shape
    count = flux_ref.shape[0]
    cells = cells_ref[...]
    stacked = split_rows(flux_ref[...])

    @pl.loop(0, width // WIDE)
    def _(at):
        first = pl.multiple_of(at * WIDE, WIDE)
        spread = lax.dot_general(
            stacked,
            one_hot(cells, first),
            (((1,), (1,)), ((), ())),
            preferred_element_type=jnp.float32,
        )
        out_ref[:, pl.ds(first, WIDE)] = joined(spread, count)[:modes]


def group_of(modes):
    return 8 if modes % 8 == 0 else 4


def mix_kernel(modes, slots, random_terms, rows, with_before, with_faces, earlier, *refs):
    previous = len(earlier)
    refs = list(refs)
    take = lambda count: [refs.pop(0) for _ in range(count)]
    partner_ref, weight_ref, coef_ref = take(3)
    parts = take(slots)
    before_ref = take(1)[0] if with_before else None
    face_coef_ref = take(1)[0] if with_faces else None
    face_parts = take(slots) if with_faces else []
    if previous:
        done = take(previous)
        uppers = take(previous)
        face_ref, alive_ref = take(2)
    out_ref, = take(1)
    if not previous:
        upper_ref, lower_ref = take(2)
    flux_ref = take(1)[0] if with_faces else None
    held, result, upper_own, lower_own = take(4)
    if with_faces:
        face_held, face_result = take(2)
    group = group_of(modes)

    size = modes * rows
    for slot, part in enumerate(parts):
        held[slot * size : (slot + 1) * size, :] = part[...]
    for slot, part in enumerate(face_parts):
        for first in range(0, modes, group):
            for row in range(4):
                face_held[pl.ds((slot * modes + first) * rows + row, group, stride=rows), :] = part[
                    first : first + group, row * GZ : (row + 1) * GZ
                ]

    row_ids = lax.broadcasted_iota(jnp.int32, (rows, GZ), 0)

    @pl.loop(0, modes // TOGETHER)
    def _(turn):
        sums = [[None] * 5 for _ in range(TOGETHER)]

        def add(at, which, value):
            old = sums[at][which]
            sums[at][which] = value if old is None else old + value

        for term in range(random_terms + 1):
            coefs = [coef_ref[which, term] for which in range(4)]
            face_coef = face_coef_ref[term] if with_faces else None
            for at in range(TOGETHER):
                mode = turn * TOGETHER + at
                if term == 0:
                    own = pl.multiple_of(mode * rows, rows)
                    mixed = held[pl.ds(own, rows), :]
                    if with_faces:
                        face_mixed = face_held[pl.ds(own, 4), :]
                else:
                    base = 2 * (term - 1)
                    one = pl.multiple_of(partner_ref[base, mode], rows)
                    two = pl.multiple_of(partner_ref[base + 1, mode], rows)
                    weight_one = weight_ref[base, mode]
                    weight_two = weight_ref[base + 1, mode]
                    mixed = weight_one * held[pl.ds(one, rows), :] + weight_two * held[pl.ds(two, rows), :]
                    if with_faces:
                        face_mixed = (
                            weight_one * face_held[pl.ds(one, 4), :]
                            + weight_two * face_held[pl.ds(two, 4), :]
                        )
                for which in range(4):
                    add(at, which, coefs[which] * mixed)
                if with_faces:
                    add(at, 4, face_coef * face_mixed)
        for at in range(TOGETHER):
            mode = turn * TOGETHER + at
            own = pl.multiple_of(mode * rows, rows)
            down, up, right, left, faces = sums[at]
            from_below = jnp.where(row_ids == rows - 1, 0.0, pltpu.roll(up, rows - 1, 0))
            from_above = jnp.where(row_ids == 0, 0.0, pltpu.roll(down, 1, 0))
            sideways = pltpu.roll(left, GZ - 1, 1) + pltpu.roll(right, 1, 1)
            result[pl.ds(own, rows), :] = (
                (down - from_below) + (up - from_above) + ((right + left) - sideways)
            )
            upper_own[pl.ds(mode, 1), :] = up[0:1]
            lower_own[pl.ds(mode, 1), :] = down[rows - 1 : rows]
            if with_faces:
                face_result[pl.ds(own, 4), :] = faces

    if with_faces:
        if flux_ref.shape[0] > modes:
            flux_ref[...] = jnp.zeros_like(flux_ref)
        for first in range(0, modes, group):
            for row in range(4):
                flux_ref[first : first + group, row * GZ : (row + 1) * GZ] = face_result[
                    pl.ds(first * rows + row, group, stride=rows), :
                ]
    offset = sum(earlier) * GZ
    for first in range(0, modes, group):
        some = slice(first, first + group)
        for row in range(rows):
            value = result[pl.ds(first * rows + row, group, stride=rows), :]
            if row == 0 and with_before:
                value = value - before_ref[some, :]
            columns = slice(offset + row * GZ, offset + (row + 1) * GZ)
            if previous:
                value = (value + face_ref[some, columns]) * alive_ref[:, columns]
            out_ref[some, columns] = value
        start = 0
        for at in range(previous):
            for row in range(earlier[at]):
                columns = slice((start + row) * GZ, (start + row + 1) * GZ)
                value = done[at][some, row * GZ : (row + 1) * GZ]
                if row == earlier[at] - 1:
                    after = uppers[at + 1] if at + 1 < previous else upper_own
                    value = value - after[some, :]
                out_ref[some, columns] = (value + face_ref[some, columns]) * alive_ref[:, columns]
            start += earlier[at]
    if not previous:
        upper_ref[...] = upper_own[...]
        lower_ref[...] = lower_own[...]


def others(count):
    return [(source, source ^ 1) for source in range(count)]


def far_modes(value):
    count = lax.axis_size("mode")
    return [
        lax.ppermute(
            value, "mode", [((target + 2 * step) % count, target) for target in range(count)]
        )
        for step in range(1, count // 2)
    ]


def with_sibling(direct):
    pieces = []
    for value in direct:
        pieces += [value, lax.ppermute(value, "mode", others(lax.axis_size("mode")))]
    return pieces


def after(values, first):
    return list(lax.optimization_barrier((values, first))[0])


def per_device(chaos_field, kl_field, partner, chaos_coef, cell_count, face_count, face_cells):
    modes, cells = chaos_field.shape
    rows_grid = cells // GZ
    sizes = chunk_rows(rows_grid)
    chunks = len(sizes)
    random_terms = partner.shape[0]
    slots = lax.axis_size("mode")
    face_limit = face_cells.shape[2]
    faces = 4 * face_limit

    raw = pl.pallas_call(
        functools.partial(relayout_kernel, sizes),
        out_shape=[jax.ShapeDtypeStruct((modes * size, GZ), jnp.float32) for size in sizes],
        in_specs=[VMEM],
        out_specs=[VMEM] * chunks,
        compiler_params=params(),
        cost_estimate=cost(1_000_000_000, 8 * modes * cells),
    )(chaos_field)
    far = [far_modes(raw[0])]
    far.append(far_modes(raw[1]))

    cells_flat = face_cells.reshape(1, faces)
    lead = -(-(random_terms + 1) // 16) * 16
    padded = -(-(lead + modes) // 16) * 16
    difference, conduct_sum = pl.pallas_call(
        functools.partial(face_kernel, lax.axis_size("blk"), lead),
        out_shape=[
            jax.ShapeDtypeStruct((modes, faces), jnp.float32),
            jax.ShapeDtypeStruct((4, lead, face_limit), jnp.float32),
        ],
        in_specs=[VMEM] * 3,
        out_specs=[VMEM] * 2,
        scratch_shapes=[
            pltpu.VMEM((padded, cells), jnp.float32),
            pltpu.VMEM((4, padded, face_limit), jnp.float32),
            pltpu.VMEM((4, padded, face_limit), jnp.float32),
            pltpu.SemaphoreType.DMA((4,)),
            pltpu.SemaphoreType.DMA((4,)),
        ],
        compiler_params=pltpu.CompilerParams(
            vmem_limit_bytes=32 * 1024 * 1024, collective_id=0, has_side_effects=True
        ),
        cost_estimate=cost(8_000_000_000, 4 * padded * cells),
    )(cells_flat, chaos_field, kl_field)
    face_alive = (
        lax.iota(jnp.int32, face_limit)[None, :] < face_count[0][:, None]
    ).astype(jnp.float32)
    face_coef = jnp.transpose(0.5 * conduct_sum * face_alive[:, None, :], (1, 0, 2))
    face_coef = face_coef[: random_terms + 1]
    far_difference = far_modes(difference)

    alive_flag = (lax.iota(jnp.int32, cells) < cell_count[0]).astype(jnp.float32)
    alive = alive_flag.reshape(rows_grid, GZ)
    conduct = kl_field.reshape(random_terms + 1, rows_grid, GZ)
    down = 0.5 * (conduct[:, 1:] + conduct[:, :-1]) * (alive[1:] * alive[:-1])
    side = 0.5 * (conduct[:, :, 1:] + conduct[:, :, :-1]) * (alive[:, 1:] * alive[:, :-1])
    coefs = jnp.stack(
        [
            jnp.pad(down, ((0, 0), (0, 1), (0, 0))),
            jnp.pad(down, ((0, 0), (1, 0), (0, 0))),
            jnp.pad(side, ((0, 0), (0, 0), (0, 1))),
            jnp.pad(side, ((0, 0), (0, 0), (1, 0))),
        ]
    )

    me = lax.axis_index("mode")
    owner = partner // modes
    step = lax.rem(owner // 2 - me // 2 + slots // 2, slots // 2)
    slot = 2 * step + ((owner ^ me) & 1)
    places = (slot * modes + lax.rem(partner, modes)).reshape(2 * random_terms, modes)
    weights = chaos_coef.reshape(2 * random_terms, modes)

    face_at = chunks - 2
    padded_modes = -(-modes // 16) * 16
    results, uppers, before, face_add = [], [], None, None
    start = 0
    for at in range(chunks):
        last = at == chunks - 1
        with_faces = at == face_at
        rows = sizes[at]
        if at + 2 < chunks:
            later = after([raw[at + 2]], [far[at], difference])[0]
            far.append(far_modes(later))
        direct = after(far[at], results[-1]) if at else far[at]
        inputs = [places * rows, weights, coefs[:, :, start : start + rows]]
        inputs += with_sibling([raw[at]] + direct)
        in_specs = [SMEM, SMEM] + [VMEM] * (1 + slots)
        if at:
            inputs.append(before)
        if with_faces:
            far_faces = after(far_difference, results[-1]) if at else far_difference
            inputs += [face_coef] + with_sibling([difference] + far_faces)
        if last:
            inputs += results + uppers + [face_add, alive_flag[None, :]]
        in_specs += [VMEM] * (len(inputs) - len(in_specs))
        edge = jax.ShapeDtypeStruct((modes, GZ), jnp.float32)
        if last:
            out_shape = [jax.ShapeDtypeStruct((modes, cells), jnp.float32)]
        else:
            out_shape = [jax.ShapeDtypeStruct((modes, rows * GZ), jnp.float32), edge, edge]
        if with_faces:
            out_shape.append(jax.ShapeDtypeStruct((padded_modes, faces), jnp.float32))
        scratch = [
            pltpu.VMEM((slots * modes * rows, GZ), jnp.float32),
            pltpu.VMEM((modes * rows, GZ), jnp.float32),
            pltpu.VMEM((modes, GZ), jnp.float32),
            pltpu.VMEM((modes, GZ), jnp.float32),
        ]
        if with_faces:
            scratch += scratch[:2]
        outs = pl.pallas_call(
            functools.partial(
                mix_kernel,
                modes,
                slots,
                random_terms,
                rows,
                at > 0,
                with_faces,
                sizes[:at] if last else [],
            ),
            out_shape=out_shape,
            in_specs=in_specs,
            out_specs=[VMEM] * len(out_shape),
            scratch_shapes=scratch,
            compiler_params=params(),
            cost_estimate=cost(6_000_000_000, 4 * slots * modes * rows * GZ),
        )(*inputs)
        if last:
            return outs[0]
        start += rows
        results.append(outs[0])
        uppers.append(outs[1])
        before = outs[2]
        if with_faces:
            face_add = pl.pallas_call(
                scatter_kernel,
                out_shape=jax.ShapeDtypeStruct((modes, cells), jnp.float32),
                in_specs=[VMEM, VMEM],
                out_specs=VMEM,
                compiler_params=params(),
                cost_estimate=cost(4_000_000_000, 4 * modes * cells),
            )(cells_flat, outs[3])


def solution(mesh):
    in_specs = (
        P("mode", "blk"),
        P(None, "blk"),
        P(None, None, "mode"),
        P(None, None, "mode"),
        P("blk"),
        P("blk", None),
        P("blk", None, None),
    )
    return jax.shard_map(
        per_device, mesh=mesh, in_specs=in_specs, out_specs=P("mode", "blk"), check_vma=False
    )
```

time: 93.6 us -> 66.9 us (0.71)
  starting transfers between devices: 19.6 us -> 8.16 us
  waiting for transfers between devices: 25.3 us -> 14.5 us
  Pallas kernels: 43 us -> 40.9 us
  local copies, waits for them, and re-layouts: 3.61 us -> 1.77 us
    ppermute x19 -> x12, starting transfers between devices: 19.6 us -> 8.16 us  [the longest x4 6.87 us: far_modes(): lax.ppermute(value, 'mode', [((target + 2 * step) % count, target) for ta...]
    ppermute x19 -> x12, waiting for transfers between devices: 25.3 us -> 14.5 us  [the longest x4 13 us: far_modes(): lax.ppermute(value, 'mode', [((target + 2 * step) % count, target) for ta...]
    pallas_call x4 -> x3, Pallas kernels: 32.6 us -> 25.5 us  [per_device(): pl.pallas_call(functools.partial(mix_kernel, modes, slots, random_terms,...]
    pallas_call x1 -> x2, Pallas kernels: 5.74 us -> 11.2 us  [the longest x1 10 us: per_device(): pl.pallas_call(functools.partial(face_kernel, lax.axis_size('blk'), lead)...]
    slice x3 -> x1, local copies, waits for them, and re-layouts: 2.44 us -> 0.01 us  [per_device(): face_coef = face_coef[:random_terms + 1]]
  transfers between devices with their start and end apart: 19 -> 12, of which waited for: 6 -> 4; matrix products, arithmetic and copies ran while one was open for 2% -> 1% of each run, Pallas kernels for 37% -> 47%
where the time goes in v2:
time: 66.9 us; the launch traced here: 66.6 us
  Pallas kernels  40.9 us (61%)
  waiting for transfers between devices  14.5 us (22%)
  starting transfers between devices  8.16 us (12%)
  local copies, waits for them, and re-layouts  1.77 us (3%)
  between operations  0.85 us (1%)
    pallas_call x3, Pallas kernels, per_device(): pl.pallas_call(functools.partial(mix_kernel, modes, slots, random_terms,...  25.5 us
    ppermute x4, waiting for transfers between devices, far_modes(): lax.ppermute(value, 'mode', [((target + 2 * step) % count, target) for ta...  13 us
    pallas_call x1, Pallas kernels, per_device(): pl.pallas_call(functools.partial(face_kernel, lax.axis_size('blk'), lead)...  10 us
    ppermute x4, starting transfers between devices, far_modes(): lax.ppermute(value, 'mode', [((target + 2 * step) % count, target) for ta...  6.87 us
    pallas_call x1, Pallas kernels, per_device(): pl.pallas_call(scatter_kernel, out_shape=jax.ShapeDtypeStruct((modes, cel...  4.21 us
    unnamed x13, local copies, waits for them, and re-layouts  1.62 us
    ppermute x8, waiting for transfers between devices, with_sibling(): lax.ppermute(value, 'mode', others(lax.axis_size('mode')))  1.52 us
  transfers between devices with their start and end apart: 12, of which 4 were waited for; matrix products, arithmetic and copies ran while one was open for 1% of the time, Pallas kernels for 47%

profile of v2, /device:TPU:0, one launch (start us, length us, event | category | flops | bytes accessed | tf_op | source)
XLA Modules:
  0.0 66.6 jit_solution(5461489969387628267)
XLA Ops:
  0.0 1.5 %copy-done.1 = f32[112,4096]{1,0:T(8,128)S(1)} copy-done((f32[112,4096]{1,0:T(8,128)S(1)}, f32[112,4096]{1,0:T(8,128)}, u32[]{:S(2)}) %copy-start.1) | copy-done | bytes 1835032
  1.5 1.2 %shard_map.73 = (f32[1792,128]{1,0:T(8,128)S(1)}, f32[896,128]{1,0:T(8,128)}, f32[896,128]{1,0:T(8,128)S(1)}) custom-call(f32[112,4096]{1,0:T(8,128)S(1)} %copy-done.1), custom_call_target="tpu_custom_call" | custom-call | flops 1000000000 | bytes 3670016 | tf_op jit(solution)/shard_map/pallas_call | solution.py:316
  2.7 3.0 %collective-permute-start.1 = (f32[1792,128]{1,0:T(8,128)S(1)}, f32[1792,128]{1,0:T(8,128)S(1)}, u32[]{:S(2)}, u32[]{:S(2)}) collective-permute-start(f32[1792,128]{1,0:T(8,128)S(1)} %get-tuple-element.22.refs_3_), channel_id=1, source_target_pairs={{2,0},{3,1},{0,2},{1,3},{6,4},{7,5},{4,6},{5,7},{10,8},{11,9},{8,1... | collective-permute-start | bytes 2752520 | tf_op jit(solution)/shard_map/ppermute | solution.py:288
  5.7 10.0 %shard_map.74 = (f32[112,512]{1,0:T(8,128)}, f32[4,16,128]{2,1,0:T(8,128)S(1)}) custom-call(s32[1,512]{1,0:T(1,128)S(1)} %bitcast.28, f32[112,4096]{1,0:T(8,128)S(1)} %copy-done.1, f32[13,4096]{1,0:T(8,128)S(1)} %copy-done), custom_call_target="tpu_custom_call" | custom-call | flops 8000000000 | bytes 2097152 | tf_op jit(solution)/shard_map/pallas_call | solution.py:330
  15.7 0.6 collective-permute-start.9
  16.3 1.5 %collective-permute-start.4 = (f32[896,128]{1,0:T(8,128)}, f32[896,128]{1,0:T(8,128)}, u32[]{:S(2)}, u32[]{:S(2)}) collective-permute-start(f32[896,128]{1,0:T(8,128)} %get-tuple-element.25.refs_3_), channel_id=1, source_target_pairs={{2,0},{3,1},{0,2},{1,3},{6,4},{7,5},{4,6},{5,7},{10,8},{11,9},{8,1... | collective-permute-start | bytes 1376264 | tf_op jit(solution)/shard_map/ppermute | solution.py:288
  18.5 0.1 copy.9
  18.6 0.1 fusion.3
  18.7 0.1 fusion
  18.8 8.0 %collective-permute-done.1.refs_5_ = f32[1792,128]{1,0:T(8,128)S(1)} collective-permute-done((f32[1792,128]{1,0:T(8,128)S(1)}, f32[1792,128]{1,0:T(8,128)S(1)}, u32[]{:S(2)}, u32[]{:S(2)}) %collective-permute-start.1) | collective-permute-done | bytes 917536 | tf_op jit(solution)/shard_map/ppermute | solution.py:288
  26.9 0.1 pad_bitcast_fusion.1
  27.1 0.1 fusion.9
  27.2 0.1 broadcast_multiply_fusion
  27.3 0.6 collective-permute-start.3
  27.8 1.5 %collective-permute-done.6.refs_6_ = f32[1792,128]{1,0:T(8,128)S(1)} collective-permute-done((f32[1792,128]{1,0:T(8,128)S(1)}, f32[1792,128]{1,0:T(8,128)S(1)}, u32[]{:S(2)}, u32[]{:S(2)}) %collective-permute-start.6) | collective-permute-done | bytes 917536 | tf_op jit(solution)/shard_map/ppermute | solution.py:298
  29.3 0.1 collective-permute-start
  29.5 7.5 %shard_map.75 = (f32[112,2048]{1,0:T(8,128)S(1)}, f32[112,128]{1,0:T(8,128)S(1)}, f32[112,128]{1,0:T(8,128)S(1)}) custom-call(s32[24,112]{1,0:T(8,128)S(1)} %bitcast.24, f32[24,112]{1,0:T(8,128)S(1)} %bitcast.25, f32[4,13,16,128]{3,2,1,0:T(8,128)S(1)} %pad_maximum_fusion.refs_2_, f32[1792,128]{1,0:T(8,128)S(1)} %get-tuple-element.22.refs_3_, ...), custom_call_target="tpu_custom_call" | custom-call | flops 6000000000 | bytes 3670016 | tf_op jit(solution)/shard_map/pallas_call | solution.py:416
  37.0 3.9 %collective-permute-done.4.refs_5_ = f32[896,128]{1,0:T(8,128)} collective-permute-done((f32[896,128]{1,0:T(8,128)}, f32[896,128]{1,0:T(8,128)}, u32[]{:S(2)}, u32[]{:S(2)}) %collective-permute-start.4) | collective-permute-done | bytes 458784 | tf_op jit(solution)/shard_map/ppermute | solution.py:288
  40.9 0.6 collective-permute-start.10
  41.6 1.8 %collective-permute-start.2 = (f32[896,128]{1,0:T(8,128)S(1)}, f32[896,128]{1,0:T(8,128)S(1)}, u32[]{:S(2)}, u32[]{:S(2)}) collective-permute-start(f32[896,128]{1,0:T(8,128)S(1)} %get-tuple-element.24.refs_3_), channel_id=1, source_target_pairs={{2,0},{3,1},{0,2},{1,3},{6,4},{7,5},{4,6},{5,7},{10,8},{11,9},{8,1... | collective-permute-start | bytes 1376264 | tf_op jit(solution)/shard_map/ppermute | solution.py:288
  43.4 9.7 %shard_map.76 = (f32[112,1024]{1,0:T(8,128)S(1)}, f32[112,128]{1,0:T(8,128)S(1)}, f32[112,128]{1,0:T(8,128)S(1)}, f32[112,512]{1,0:T(8,128)S(1)}) custom-call(s32[24,112]{1,0:T(8,128)S(1)} %bitcast.22, f32[24,112]{1,0:T(8,128)S(1)} %bitcast.26, f32[4,13,8,128]{3,2,1,0:T(8,128)S(1)} %get-tuple-element.39.refs_2_, f32[896,128]{1,0:T(8,128)} %get-tuple-element.25.refs_3_, ...), custom_call_target="tpu_custom_call" | custom-call | flops 6000000000 | bytes 1835008 | tf_op jit(solution)/shard_map/pallas_call | solution.py:416
  53.1 1.0 %collective-permute-done.2.refs_5_ = f32[896,128]{1,0:T(8,128)S(1)} collective-permute-done((f32[896,128]{1,0:T(8,128)S(1)}, f32[896,128]{1,0:T(8,128)S(1)}, u32[]{:S(2)}, u32[]{:S(2)}) %collective-permute-start.2) | collective-permute-done | bytes 458784 | tf_op jit(solution)/shard_map/ppermute | solution.py:288
  54.1 4.2 %shard_map.77.refs_12_ = f32[112,4096]{1,0:T(8,128)S(1)} custom-call(s32[1,512]{1,0:T(1,128)S(1)} %bitcast.29, f32[112,512]{1,0:T(8,128)S(1)} %get-tuple-element.36.flux_ref), custom_call_target="tpu_custom_call" | custom-call | flops 4000000000 | bytes 1835008 | tf_op jit(solution)/shard_map/pallas_call | solution.py:441
  58.3 8.3 %shard_map.78 = f32[112,4096]{1,0:T(8,128)} custom-call(s32[24,112]{1,0:T(8,128)S(1)} %bitcast.23, f32[24,112]{1,0:T(8,128)S(1)} %bitcast.27, f32[4,13,8,128]{3,2,1,0:T(8,128)S(1)} %get-tuple-element.40.refs_2_, f32[896,128]{1,0:T(8,128)S(1)} %get-tuple-element.24.refs_3_, f32[896,128]{1,0:T(8,128)S(1)} %collective-permute-done.refs_4_, ...), custom_call_target="tpu_custom_call" | custom-call | flops 6000000000 | bytes 1835008 | tf_op jit(solution)/shard_map/pallas_call | solution.py:416
  (34 shorter events, 0.2 us)
Async XLA Ops:
  0.0 5.7 %copy-start = (f32[13,4096]{1,0:T(8,128)S(1)}, f32[13,4096]{1,0:T(8,128)}, u32[]{:S(2)}) copy-start(f32[13,4096]{1,0:T(8,128)} %kl_ref.1) | copy-start | bytes 638980
  0.0 1.5 %copy-start.1 = (f32[112,4096]{1,0:T(8,128)S(1)}, f32[112,4096]{1,0:T(8,128)}, u32[]{:S(2)}) copy-start(f32[112,4096]{1,0:T(8,128)} %field_ref.3) | copy-start | bytes 5505028
  1.5 4.2 %copy-start.3 = (s32[1,4,128]{2,1,0:T(4,128)S(1)}, s32[1,4,128]{2,1,0:T(4,128)}, u32[]{:S(2)}) copy-start(s32[1,4,128]{2,1,0:T(4,128)} %param.13) | copy-start | bytes 6148
  2.7 24.1 %collective-permute-start.1 = (f32[1792,128]{1,0:T(8,128)S(1)}, f32[1792,128]{1,0:T(8,128)S(1)}, u32[]{:S(2)}, u32[]{:S(2)}) collective-permute-start(f32[1792,128]{1,0:T(8,128)S(1)} %get-tuple-element.22.refs_3_), channel_id=1, source_target_pairs={{2,0},{3,1},{0,2},{1,3},{6,4},{7,5},{4,6},{5,7},{10,8},{11,9},{8,1... | collective-permute-start | bytes 2752520 | tf_op jit(solution)/shard_map/ppermute | solution.py:288
  5.7 21.6 %collective-permute-start.5 = (f32[1792,128]{1,0:T(8,128)S(1)}, f32[1792,128]{1,0:T(8,128)S(1)}, u32[]{:S(2)}, u32[]{:S(2)}) collective-permute-start(f32[1792,128]{1,0:T(8,128)S(1)} %get-tuple-element.22.refs_3_), channel_id=1, source_target_pairs={{0,1},{1,0},{2,3},{3,2},{4,5},{5,4},{6,7},{7,6},{8,9},{9,8},{10,11... | collective-permute-start | bytes 2752520 | tf_op jit(solution)/shard_map/ppermute | solution.py:298
  15.7 25.2 %collective-permute-start.9 = (f32[112,512]{1,0:T(8,128)}, f32[112,512]{1,0:T(8,128)}, u32[]{:S(2)}, u32[]{:S(2)}) collective-permute-start(f32[112,512]{1,0:T(8,128)} %get-tuple-element.23.refs_9_), channel_id=1, source_target_pairs={{2,0},{3,1},{0,2},{1,3},{6,4},{7,5},{4,6},{5,7},{10,8},{11,9},{8,1... | collective-permute-start | bytes 688136 | tf_op jit(solution)/shard_map/ppermute | solution.py:288
  16.3 25.2 %collective-permute-start.8 = (f32[112,512]{1,0:T(8,128)}, f32[112,512]{1,0:T(8,128)}, u32[]{:S(2)}, u32[]{:S(2)}) collective-permute-start(f32[112,512]{1,0:T(8,128)} %get-tuple-element.23.refs_9_), channel_id=1, source_target_pairs={{0,1},{1,0},{2,3},{3,2},{4,5},{5,4},{6,7},{7,6},{8,9},{9,8},{10,11... | collective-permute-start | bytes 688136 | tf_op jit(solution)/shard_map/ppermute | solution.py:298
  16.3 24.6 %collective-permute-start.4 = (f32[896,128]{1,0:T(8,128)}, f32[896,128]{1,0:T(8,128)}, u32[]{:S(2)}, u32[]{:S(2)}) collective-permute-start(f32[896,128]{1,0:T(8,128)} %get-tuple-element.25.refs_3_), channel_id=1, source_target_pairs={{2,0},{3,1},{0,2},{1,3},{6,4},{7,5},{4,6},{5,7},{10,8},{11,9},{8,1... | collective-permute-start | bytes 1376264 | tf_op jit(solution)/shard_map/ppermute | solution.py:288
  18.7 8.4 %copy-start.5 = (s32[1,4]{1,0:T(1,128)S(1)}, s32[1,4]{1,0:T(1,128)}, u32[]{:S(2)}) copy-start(s32[1,4]{1,0:T(1,128)} %param.12) | copy-start | bytes 52
  18.7 8.5 %copy-start.4 = (s32[12,2,112]{2,1,0:T(2,128)S(1)}, s32[12,2,112]{2,1,0:T(2,128)}, u32[]{:S(2)}) copy-start(s32[12,2,112]{2,1,0:T(2,128)} %param.9) | copy-start | bytes 32260
  18.7 10.8 %copy-start.2 = (f32[12,2,112]{2,1,0:T(2,128)S(1)}, f32[12,2,112]{2,1,0:T(2,128)}, u32[]{:S(2)}) copy-start(f32[12,2,112]{2,1,0:T(2,128)} %param.10) | copy-start | bytes 32260
  26.9 2.5 %collective-permute-start.6 = (f32[1792,128]{1,0:T(8,128)S(1)}, f32[1792,128]{1,0:T(8,128)S(1)}, u32[]{:S(2)}, u32[]{:S(2)}) collective-permute-start(f32[1792,128]{1,0:T(8,128)S(1)} %collective-permute-done.1.refs_5_), channel_id=1, source_target_pairs={{0,1},{1,0},{2,3},{3,2},{4,5},{5,4},{6,7},{7,6},{8,9},{9,8},{10,11... | collective-permute-start | bytes 2752520 | tf_op jit(solution)/shard_map/ppermute | solution.py:298
  27.3 16.1 %collective-permute-start.3 = (f32[896,128]{1,0:T(8,128)}, f32[896,128]{1,0:T(8,128)S(1)}, u32[]{:S(2)}, u32[]{:S(2)}) collective-permute-start(f32[896,128]{1,0:T(8,128)} %get-tuple-element.25.refs_3_), channel_id=1, source_target_pairs={{0,1},{1,0},{2,3},{3,2},{4,5},{5,4},{6,7},{7,6},{8,9},{9,8},{10,11... | collective-permute-start | bytes 1376264 | tf_op jit(solution)/shard_map/ppermute | solution.py:298
  29.3 29.0 %collective-permute-start = (f32[896,128]{1,0:T(8,128)S(1)}, f32[896,128]{1,0:T(8,128)S(1)}, u32[]{:S(2)}, u32[]{:S(2)}) collective-permute-start(f32[896,128]{1,0:T(8,128)S(1)} %get-tuple-element.24.refs_3_), channel_id=1, source_target_pairs={{0,1},{1,0},{2,3},{3,2},{4,5},{5,4},{6,7},{7,6},{8,9},{9,8},{10,11... | collective-permute-start | bytes 1376264 | tf_op jit(solution)/shard_map/ppermute | solution.py:298
  40.9 2.5 %collective-permute-start.7 = (f32[896,128]{1,0:T(8,128)}, f32[896,128]{1,0:T(8,128)S(1)}, u32[]{:S(2)}, u32[]{:S(2)}) collective-permute-start(f32[896,128]{1,0:T(8,128)} %collective-permute-done.4.refs_5_), channel_id=1, source_target_pairs={{0,1},{1,0},{2,3},{3,2},{4,5},{5,4},{6,7},{7,6},{8,9},{9,8},{10,11... | collective-permute-start | bytes 1376264 | tf_op jit(solution)/shard_map/ppermute | solution.py:298
  40.9 2.5 %collective-permute-start.10 = (f32[112,512]{1,0:T(8,128)}, f32[112,512]{1,0:T(8,128)S(1)}, u32[]{:S(2)}, u32[]{:S(2)}) collective-permute-start(f32[112,512]{1,0:T(8,128)} %collective-permute-done.9.refs_11_), channel_id=1, source_target_pairs={{0,1},{1,0},{2,3},{3,2},{4,5},{5,4},{6,7},{7,6},{8,9},{9,8},{10,11... | collective-permute-start | bytes 688136 | tf_op jit(solution)/shard_map/ppermute | solution.py:298
  41.6 12.5 %collective-permute-start.2 = (f32[896,128]{1,0:T(8,128)S(1)}, f32[896,128]{1,0:T(8,128)S(1)}, u32[]{:S(2)}, u32[]{:S(2)}) collective-permute-start(f32[896,128]{1,0:T(8,128)S(1)} %get-tuple-element.24.refs_3_), channel_id=1, source_target_pairs={{2,0},{3,1},{0,2},{1,3},{6,4},{7,5},{4,6},{5,7},{10,8},{11,9},{8,1... | collective-permute-start | bytes 1376264 | tf_op jit(solution)/shard_map/ppermute | solution.py:288
  54.1 4.3 %collective-permute-start.11 = (f32[896,128]{1,0:T(8,128)S(1)}, f32[896,128]{1,0:T(8,128)S(1)}, u32[]{:S(2)}, u32[]{:S(2)}) collective-permute-start(f32[896,128]{1,0:T(8,128)S(1)} %collective-permute-done.2.refs_5_), channel_id=1, source_target_pairs={{0,1},{1,0},{2,3},{3,2},{4,5},{5,4},{6,7},{7,6},{8,9},{9,8},{10,11... | collective-permute-start | bytes 1376264 | tf_op jit(solution)/shard_map/ppermute | solution.py:298

commit v3 on v2

--- a/solution.py
+++ b/solution.py
@@ -41,8 +41,7 @@
 
 def chunk_rows(rows_grid):
     half = rows_grid // 2 // TILE * TILE
-    rest = rows_grid - half
-    return [half] + [TILE] * (rest // TILE)
+    return [half, rows_grid - half]
 
 
 def relayout_kernel(sizes, field_ref, *out_refs):
@@ -215,10 +214,10 @@
                         face_mixed = face_held[pl.ds(own, 4), :]
                 else:
                     base = 2 * (term - 1)
-                    one = pl.multiple_of(partner_ref[base, mode], rows)
-                    two = pl.multiple_of(partner_ref[base + 1, mode], rows)
-                    weight_one = weight_ref[base, mode]
-                    weight_two = weight_ref[base + 1, mode]
+                    one = pl.multiple_of(partner_ref[mode * (2 * random_terms) + base], rows)
+                    two = pl.multiple_of(partner_ref[mode * (2 * random_terms) + base + 1], rows)
+                    weight_one = weight_ref[mode, base : base + 1, :]
+                    weight_two = weight_ref[mode, base + 1 : base + 2, :]
                     mixed = weight_one * held[pl.ds(one, rows), :] + weight_two * held[pl.ds(two, rows), :]
                     if with_faces:
                         face_mixed = (
@@ -322,9 +321,9 @@
         cost_estimate=cost(1_000_000_000, 8 * modes * cells),
     )(chaos_field)
     far = [far_modes(raw[0])]
-    far.append(far_modes(raw[1]))
-
-    cells_flat = face_cells.reshape(1, faces)
+    far.append(far_modes(after([raw[1]], far[0])[0]))
+
+    cells_flat = after([face_cells.reshape(1, faces)], raw[0])[0]
     lead = -(-(random_terms + 1) // 16) * 16
     padded = -(-(lead + modes) // 16) * 16
     difference, conduct_sum = pl.pallas_call(
@@ -373,7 +372,9 @@
     step = lax.rem(owner // 2 - me // 2 + slots // 2, slots // 2)
     slot = 2 * step + ((owner ^ me) & 1)
     places = (slot * modes + lax.rem(partner, modes)).reshape(2 * random_terms, modes)
-    weights = chaos_coef.reshape(2 * random_terms, modes)
+    places = places.T.reshape(-1)
+    weights = chaos_coef.reshape(2 * random_terms, modes).T
+    weights = jnp.broadcast_to(weights[:, :, None], weights.shape + (GZ,))
 
     face_at = chunks - 2
     padded_modes = -(-modes // 16) * 16
@@ -386,10 +387,10 @@
         if at + 2 < chunks:
             later = after([raw[at + 2]], [far[at], difference])[0]
             far.append(far_modes(later))
-        direct = after(far[at], results[-1]) if at else far[at]
+        direct = after(far[at], face_add if last else results[-1]) if at else far[at]
         inputs = [places * rows, weights, coefs[:, :, start : start + rows]]
         inputs += with_sibling([raw[at]] + direct)
-        in_specs = [SMEM, SMEM] + [VMEM] * (1 + slots)
+        in_specs = [SMEM] + [VMEM] * (2 + slots)
         if at:
             inputs.append(before)
         if with_faces:

time: 66.9 us -> 74.7 us (1.12); the launches traced: 66.6 us -> 73.6 us
  waiting for transfers between devices: 14.5 us -> 28.6 us
  Pallas kernels: 40.9 us -> 34.8 us
  starting transfers between devices: 8.16 us -> 4.76 us
  local copies, waits for them, and re-layouts: 1.77 us -> 4.11 us
    ppermute x4 -> x3, waiting for transfers between devices: 13 us -> 25.9 us  [far_modes(): lax.ppermute(value, 'mode', [((target + 2 * step) % count, target) for ta...]
    pallas_call x3 -> x2, Pallas kernels: 25.5 us -> 19.5 us  [per_device(): pl.pallas_call(functools.partial(mix_kernel, modes, slots, random_terms,...]
    ppermute x4 -> x3, starting transfers between devices: 6.87 us -> 3.67 us  [far_modes(): lax.ppermute(value, 'mode', [((target + 2 * step) % count, target) for ta...]
    mul x0 -> x2, local copies, waits for them, and re-layouts: none -> 1.62 us  [per_device(): inputs = [places * rows, weights, coefs[:, :, start:start + rows]]]
    ppermute x8 -> x6, waiting for transfers between devices: 1.52 us -> 2.75 us  [with_sibling(): lax.ppermute(value, 'mode', others(lax.axis_size('mode')))]
  transfers between devices with their start and end apart: 12 -> 9, of which waited for: 4 -> 4; matrix products, arithmetic and copies ran while one was open for 1% -> 4% of each run, Pallas kernels for 47% -> 20%
where the time goes in v3:
time: 74.7 us; the launch traced here: 73.6 us
  Pallas kernels  34.8 us (47%)
  waiting for transfers between devices  28.6 us (38%)
  starting transfers between devices  4.76 us (6%)
  local copies, waits for them, and re-layouts  4.11 us (6%)
  between operations  0.82 us (1%)
    ppermute x3, waiting for transfers between devices, far_modes(): lax.ppermute(value, 'mode', [((target + 2 * step) % count, target) for ta...  25.9 us
    pallas_call x2, Pallas kernels, per_device(): pl.pallas_call(functools.partial(mix_kernel, modes, slots, random_terms,...  19.5 us
    pallas_call x1, Pallas kernels, per_device(): pl.pallas_call(functools.partial(face_kernel, lax.axis_size('blk'), lead)...  10.6 us
    pallas_call x1, Pallas kernels, per_device(): pl.pallas_call(scatter_kernel, out_shape=jax.ShapeDtypeStruct((modes, cel...  4.21 us
    ppermute x3, starting transfers between devices, far_modes(): lax.ppermute(value, 'mode', [((target + 2 * step) % count, target) for ta...  3.67 us
    ppermute x6, waiting for transfers between devices, with_sibling(): lax.ppermute(value, 'mode', others(lax.axis_size('mode')))  2.75 us
    unnamed x13, local copies, waits for them, and re-layouts  1.77 us
    mul x2, local copies, waits for them, and re-layouts, per_device(): inputs = [places * rows, weights, coefs[:, :, start:start + rows]]  1.62 us
  transfers between devices with their start and end apart: 9, of which 4 were waited for; matrix products, arithmetic and copies ran while one was open for 4% of the time, Pallas kernels for 20%

profile of v3, /device:TPU:0, one launch (start us, length us, event | category | flops | bytes accessed | tf_op | source)
XLA Modules:
  0.0 73.6 jit_solution(12058427381976885179)
XLA Ops:
  0.0 1.5 %copy-done.1 = f32[112,4096]{1,0:T(8,128)S(1)} copy-done((f32[112,4096]{1,0:T(8,128)S(1)}, f32[112,4096]{1,0:T(8,128)}, u32[]{:S(2)}) %copy-start.1) | copy-done | bytes 1835032
  1.5 0.5 shard_map.73
  2.1 0.2 copy-done.2
  2.2 10.6 %shard_map.74 = (f32[112,512]{1,0:T(8,128)S(1)}, f32[4,16,128]{2,1,0:T(8,128)S(1)}) custom-call(s32[1,512]{1,0:T(1,128)S(1)} %bitcast.23, f32[112,4096]{1,0:T(8,128)S(1)} %copy-done.1, f32[13,4096]{1,0:T(8,128)S(1)} %copy-done), custom_call_target="tpu_custom_call" | custom-call | flops 8000000000 | bytes 2097152 | tf_op jit(solution)/shard_map/pallas_call | solution.py:329
  12.8 1.6 %collective-permute-start.6 = (f32[112,512]{1,0:T(8,128)S(1)}, f32[112,512]{1,0:T(8,128)S(1)}, u32[]{:S(2)}, u32[]{:S(2)}) collective-permute-start(f32[112,512]{1,0:T(8,128)S(1)} %get-tuple-element.21.refs_8_), channel_id=1, source_target_pairs={{2,0},{3,1},{0,2},{1,3},{6,4},{7,5},{4,6},{5,7},{10,8},{11,9},{8,1... | collective-permute-start | bytes 688136 | tf_op jit(solution)/shard_map/ppermute | solution.py:287
  14.4 0.5 collective-permute-start.1
  14.9 0.2 collective-permute-start.3
  15.1 0.3 collective-permute-start
  15.4 0.1 add_multiply_fusion
  15.5 0.7 copy.10
  16.2 0.9 %mul.69.refs_0_ = s32[2688]{0:T(1024)S(1)} reshape(s32[112,24]{1,0:T(8,128)} %bitcast.26) | data formatting | bytes 21504 | tf_op jit(solution)/shard_map/mul | solution.py:391
  18.0 0.1 copy.11
  18.2 0.1 fusion
  18.3 20.3 %collective-permute-done.1.refs_5_ = f32[1792,128]{1,0:T(8,128)} collective-permute-done((f32[1792,128]{1,0:T(8,128)S(1)}, f32[1792,128]{1,0:T(8,128)}, u32[]{:S(2)}, u32[]{:S(2)}) %collective-permute-start.1) | collective-permute-done | bytes 917536 | tf_op jit(solution)/shard_map/ppermute | solution.py:287
  38.7 0.1 pad_bitcast_fusion.1
  38.9 0.6 collective-permute-start.7
  39.6 1.6 %collective-permute-start.2 = (f32[1792,128]{1,0:T(8,128)S(1)}, f32[1792,128]{1,0:T(8,128)S(1)}, u32[]{:S(2)}, u32[]{:S(2)}) collective-permute-start(f32[1792,128]{1,0:T(8,128)S(1)} %get-tuple-element.18.refs_3_), channel_id=1, source_target_pairs={{2,0},{3,1},{0,2},{1,3},{6,4},{7,5},{4,6},{5,7},{10,8},{11,9},{8,1... | collective-permute-start | bytes 2752520 | tf_op jit(solution)/shard_map/ppermute | solution.py:287
  41.2 0.3 collective-permute-done.7.refs_11_
  41.5 0.4 broadcast_in_dim.2.refs_1_
  41.9 10.3 %shard_map.75 = (f32[112,2048]{1,0:T(8,128)S(1)}, f32[112,128]{1,0:T(8,128)S(1)}, f32[112,128]{1,0:T(8,128)S(1)}, f32[112,512]{1,0:T(8,128)S(1)}) custom-call(s32[2688]{0:T(1024)S(1)} %mul.69.refs_0_, f32[112,24,128]{2,1,0:T(8,128)S(1)} %broadcast_in_dim.2.refs_1_, f32[4,13,16,128]{3,2,1,0:T(8,128)S(1)} %get-tuple-element.27.refs_2_, ...), custom_call_target="tpu_custom_call" | custom-call | flops 6000000000 | bytes 3670016 | tf_op jit(solution)/shard_map/pallas_call | solution.py:417
  52.2 4.2 %shard_map.76.refs_10_ = f32[112,4096]{1,0:T(8,128)S(1)} custom-call(s32[1,512]{1,0:T(1,128)S(1)} %bitcast.24, f32[112,512]{1,0:T(8,128)S(1)} %get-tuple-element.22.flux_ref), custom_call_target="tpu_custom_call" | custom-call | flops 4000000000 | bytes 1835008 | tf_op jit(solution)/shard_map/pallas_call | solution.py:442
  56.4 5.5 %collective-permute-done.2.refs_5_ = f32[1792,128]{1,0:T(8,128)S(1)} collective-permute-done((f32[1792,128]{1,0:T(8,128)S(1)}, f32[1792,128]{1,0:T(8,128)S(1)}, u32[]{:S(2)}, u32[]{:S(2)}) %collective-permute-start.2) | collective-permute-done | bytes 917536 | tf_op jit(solution)/shard_map/ppermute | solution.py:287
  62.0 2.4 %collective-permute-done.8.refs_6_ = f32[1792,128]{1,0:T(8,128)S(1)} collective-permute-done((f32[1792,128]{1,0:T(8,128)S(1)}, f32[1792,128]{1,0:T(8,128)S(1)}, u32[]{:S(2)}, u32[]{:S(2)}) %collective-permute-start.8) | collective-permute-done | bytes 917536 | tf_op jit(solution)/shard_map/ppermute | solution.py:297
  64.4 9.3 %shard_map.77 = f32[112,4096]{1,0:T(8,128)} custom-call(s32[2688]{0:T(1024)S(1)} %mul.69.refs_0_, f32[112,24,128]{2,1,0:T(8,128)S(1)} %broadcast_in_dim.2.refs_1_, f32[4,13,16,128]{3,2,1,0:T(8,128)S(1)} %get-tuple-element.28.refs_2_, f32[1792,128]{1,0:T(8,128)S(1)} %get-tuple-element.18.refs_3_, f32[1792,128]{1,0:T(8,128)S(1)} %collective-permute-done.refs_4_, ...), custom_call_target="tpu_custom_call" | custom-call | flops 6000000000 | bytes 3670016 | tf_op jit(solution)/shard_map/pallas_call | solution.py:417
  (30 shorter events, 0.5 us)
Async XLA Ops:
  0.0 2.1 %copy-start = (f32[13,4096]{1,0:T(8,128)S(1)}, f32[13,4096]{1,0:T(8,128)}, u32[]{:S(2)}) copy-start(f32[13,4096]{1,0:T(8,128)} %kl_ref.1) | copy-start | bytes 638980
  0.0 1.5 %copy-start.1 = (f32[112,4096]{1,0:T(8,128)S(1)}, f32[112,4096]{1,0:T(8,128)}, u32[]{:S(2)}) copy-start(f32[112,4096]{1,0:T(8,128)} %field_ref.3) | copy-start | bytes 5505028
  1.5 0.7 copy-start.2
  2.2 13.2 %copy-start.3 = (s32[12,2,112]{2,1,0:T(2,128)S(1)}, s32[12,2,112]{2,1,0:T(2,128)}, u32[]{:S(2)}) copy-start(s32[12,2,112]{2,1,0:T(2,128)} %param.9) | copy-start | bytes 32260
  2.2 15.7 %copy-start.5 = (s32[1,4]{1,0:T(1,128)S(1)}, s32[1,4]{1,0:T(1,128)}, u32[]{:S(2)}) copy-start(s32[1,4]{1,0:T(1,128)} %param.12) | copy-start | bytes 52
  2.2 15.8 %copy-start.4 = (f32[12,2,112]{2,1,0:T(2,128)S(1)}, f32[12,2,112]{2,1,0:T(2,128)}, u32[]{:S(2)}) copy-start(f32[12,2,112]{2,1,0:T(2,128)} %param.10) | copy-start | bytes 32260
  12.8 26.1 %collective-permute-start.6 = (f32[112,512]{1,0:T(8,128)S(1)}, f32[112,512]{1,0:T(8,128)S(1)}, u32[]{:S(2)}, u32[]{:S(2)}) collective-permute-start(f32[112,512]{1,0:T(8,128)S(1)} %get-tuple-element.21.refs_8_), channel_id=1, source_target_pairs={{2,0},{3,1},{0,2},{1,3},{6,4},{7,5},{4,6},{5,7},{10,8},{11,9},{8,1... | collective-permute-start | bytes 688136 | tf_op jit(solution)/shard_map/ppermute | solution.py:287
  14.4 25.2 %collective-permute-start.5 = (f32[112,512]{1,0:T(8,128)S(1)}, f32[112,512]{1,0:T(8,128)}, u32[]{:S(2)}, u32[]{:S(2)}) collective-permute-start(f32[112,512]{1,0:T(8,128)S(1)} %get-tuple-element.21.refs_8_), channel_id=1, source_target_pairs={{0,1},{1,0},{2,3},{3,2},{4,5},{5,4},{6,7},{7,6},{8,9},{9,8},{10,11... | collective-permute-start | bytes 688136 | tf_op jit(solution)/shard_map/ppermute | solution.py:297
  14.4 24.3 %collective-permute-start.1 = (f32[1792,128]{1,0:T(8,128)S(1)}, f32[1792,128]{1,0:T(8,128)}, u32[]{:S(2)}, u32[]{:S(2)}) collective-permute-start(f32[1792,128]{1,0:T(8,128)S(1)} %get-tuple-element.17.refs_3_), channel_id=1, source_target_pairs={{2,0},{3,1},{0,2},{1,3},{6,4},{7,5},{4,6},{5,7},{10,8},{11,9},{8,1... | collective-permute-start | bytes 2752520 | tf_op jit(solution)/shard_map/ppermute | solution.py:287
  14.9 26.6 %collective-permute-start.3 = (f32[1792,128]{1,0:T(8,128)S(1)}, f32[1792,128]{1,0:T(8,128)}, u32[]{:S(2)}, u32[]{:S(2)}) collective-permute-start(f32[1792,128]{1,0:T(8,128)S(1)} %get-tuple-element.17.refs_3_), channel_id=1, source_target_pairs={{0,1},{1,0},{2,3},{3,2},{4,5},{5,4},{6,7},{7,6},{8,9},{9,8},{10,11... | collective-permute-start | bytes 2752520 | tf_op jit(solution)/shard_map/ppermute | solution.py:297
  15.1 46.8 %collective-permute-start = (f32[1792,128]{1,0:T(8,128)S(1)}, f32[1792,128]{1,0:T(8,128)S(1)}, u32[]{:S(2)}, u32[]{:S(2)}) collective-permute-start(f32[1792,128]{1,0:T(8,128)S(1)} %get-tuple-element.18.refs_3_), channel_id=1, source_target_pairs={{0,1},{1,0},{2,3},{3,2},{4,5},{5,4},{6,7},{7,6},{8,9},{9,8},{10,11... | collective-permute-start | bytes 2752520 | tf_op jit(solution)/shard_map/ppermute | solution.py:297
  38.7 2.8 %collective-permute-start.4 = (f32[1792,128]{1,0:T(8,128)}, f32[1792,128]{1,0:T(8,128)S(1)}, u32[]{:S(2)}, u32[]{:S(2)}) collective-permute-start(f32[1792,128]{1,0:T(8,128)} %collective-permute-done.1.refs_5_), channel_id=1, source_target_pairs={{0,1},{1,0},{2,3},{3,2},{4,5},{5,4},{6,7},{7,6},{8,9},{9,8},{10,11... | collective-permute-start | bytes 2752520 | tf_op jit(solution)/shard_map/ppermute | solution.py:297
  38.9 2.5 %collective-permute-start.7 = (f32[112,512]{1,0:T(8,128)S(1)}, f32[112,512]{1,0:T(8,128)S(1)}, u32[]{:S(2)}, u32[]{:S(2)}) collective-permute-start(f32[112,512]{1,0:T(8,128)S(1)} %collective-permute-done.6.refs_10_), channel_id=1, source_target_pairs={{0,1},{1,0},{2,3},{3,2},{4,5},{5,4},{6,7},{7,6},{8,9},{9,8},{10,11... | collective-permute-start | bytes 688136 | tf_op jit(solution)/shard_map/ppermute | solution.py:297
  39.6 22.3 %collective-permute-start.2 = (f32[1792,128]{1,0:T(8,128)S(1)}, f32[1792,128]{1,0:T(8,128)S(1)}, u32[]{:S(2)}, u32[]{:S(2)}) collective-permute-start(f32[1792,128]{1,0:T(8,128)S(1)} %get-tuple-element.18.refs_3_), channel_id=1, source_target_pairs={{2,0},{3,1},{0,2},{1,3},{6,4},{7,5},{4,6},{5,7},{10,8},{11,9},{8,1... | collective-permute-start | bytes 2752520 | tf_op jit(solution)/shard_map/ppermute | solution.py:287
  61.9 2.5 %collective-permute-start.8 = (f32[1792,128]{1,0:T(8,128)S(1)}, f32[1792,128]{1,0:T(8,128)S(1)}, u32[]{:S(2)}, u32[]{:S(2)}) collective-permute-start(f32[1792,128]{1,0:T(8,128)S(1)} %collective-permute-done.2.refs_5_), channel_id=1, source_target_pairs={{0,1},{1,0},{2,3},{3,2},{4,5},{5,4},{6,7},{7,6},{8,9},{9,8},{10,11... | collective-permute-start | bytes 2752520 | tf_op jit(solution)/shard_map/ppermute | solution.py:297

commit v4 on v3

--- a/solution.py
+++ b/solution.py
@@ -216,8 +216,8 @@
                     base = 2 * (term - 1)
                     one = pl.multiple_of(partner_ref[mode * (2 * random_terms) + base], rows)
                     two = pl.multiple_of(partner_ref[mode * (2 * random_terms) + base + 1], rows)
-                    weight_one = weight_ref[mode, base : base + 1, :]
-                    weight_two = weight_ref[mode, base + 1 : base + 2, :]
+                    weight_one = weight_ref[mode * (2 * random_terms) + base]
+                    weight_two = weight_ref[mode * (2 * random_terms) + base + 1]
                     mixed = weight_one * held[pl.ds(one, rows), :] + weight_two * held[pl.ds(two, rows), :]
                     if with_faces:
                         face_mixed = (
@@ -321,7 +321,6 @@
         cost_estimate=cost(1_000_000_000, 8 * modes * cells),
     )(chaos_field)
     far = [far_modes(raw[0])]
-    far.append(far_modes(after([raw[1]], far[0])[0]))
 
     cells_flat = after([face_cells.reshape(1, faces)], raw[0])[0]
     lead = -(-(random_terms + 1) // 16) * 16
@@ -351,7 +350,9 @@
     ).astype(jnp.float32)
     face_coef = jnp.transpose(0.5 * conduct_sum * face_alive[:, None, :], (1, 0, 2))
     face_coef = face_coef[: random_terms + 1]
-    far_difference = far_modes(difference)
+    held_difference, held_next = after([difference, raw[1]], far[0])
+    far_difference = far_modes(held_difference)
+    far.append(far_modes(held_next))
 
     alive_flag = (lax.iota(jnp.int32, cells) < cell_count[0]).astype(jnp.float32)
     alive = alive_flag.reshape(rows_grid, GZ)
@@ -373,8 +374,7 @@
     slot = 2 * step + ((owner ^ me) & 1)
     places = (slot * modes + lax.rem(partner, modes)).reshape(2 * random_terms, modes)
     places = places.T.reshape(-1)
-    weights = chaos_coef.reshape(2 * random_terms, modes).T
-    weights = jnp.broadcast_to(weights[:, :, None], weights.shape + (GZ,))
+    weights = chaos_coef.reshape(2 * random_terms, modes).T.reshape(-1)
 
     face_at = chunks - 2
     padded_modes = -(-modes // 16) * 16
@@ -390,7 +390,7 @@
         direct = after(far[at], face_add if last else results[-1]) if at else far[at]
         inputs = [places * rows, weights, coefs[:, :, start : start + rows]]
         inputs += with_sibling([raw[at]] + direct)
-        in_specs = [SMEM] + [VMEM] * (2 + slots)
+        in_specs = [SMEM, SMEM] + [VMEM] * (1 + slots)
         if at:
             inputs.append(before)
         if with_faces:

time: 74.7 us -> 67.8 us (0.908); the launches traced: 73.6 us -> 67.5 us
  waiting for transfers between devices: 28.6 us -> 23 us
  Pallas kernels: 34.8 us -> 32.3 us
  starting transfers between devices: 4.76 us -> 7.22 us
    ppermute x3, waiting for transfers between devices: 25.9 us -> 20.6 us  [far_modes(): lax.ppermute(value, 'mode', [((target + 2 * step) % count, target) for ta...]
    ppermute x3, starting transfers between devices: 3.67 us -> 6.64 us  [far_modes(): lax.ppermute(value, 'mode', [((target + 2 * step) % count, target) for ta...]
    pallas_call x2, Pallas kernels: 19.5 us -> 18.3 us  [per_device(): pl.pallas_call(functools.partial(mix_kernel, modes, slots, random_terms,...]
    pallas_call x1, Pallas kernels: 10.6 us -> 9.35 us  [per_device(): pl.pallas_call(functools.partial(face_kernel, lax.axis_size('blk'), lead)...]
  transfers between devices with their start and end apart: 9 -> 9, of which waited for: 4 -> 4; matrix products, arithmetic and copies ran while one was open for 4% -> 4% of each run, Pallas kernels for 20% -> 35%
where the time goes in v4:
time: 67.8 us; the launch traced here: 67.5 us
  Pallas kernels  32.3 us (48%)
  waiting for transfers between devices  23 us (34%)
  starting transfers between devices  7.22 us (11%)
  local copies, waits for them, and re-layouts  3.64 us (5%)
  between operations  0.84 us (1%)
    ppermute x3, waiting for transfers between devices, far_modes(): lax.ppermute(value, 'mode', [((target + 2 * step) % count, target) for ta...  20.6 us
    pallas_call x2, Pallas kernels, per_device(): pl.pallas_call(functools.partial(mix_kernel, modes, slots, random_terms,...  18.3 us
    pallas_call x1, Pallas kernels, per_device(): pl.pallas_call(functools.partial(face_kernel, lax.axis_size('blk'), lead)...  9.35 us
    ppermute x3, starting transfers between devices, far_modes(): lax.ppermute(value, 'mode', [((target + 2 * step) % count, target) for ta...  6.64 us
    pallas_call x1, Pallas kernels, per_device(): pl.pallas_call(scatter_kernel, out_shape=jax.ShapeDtypeStruct((modes, cel...  4.21 us
    ppermute x6, waiting for transfers between devices, with_sibling(): lax.ppermute(value, 'mode', others(lax.axis_size('mode')))  2.45 us
    unnamed x13, local copies, waits for them, and re-layouts  1.62 us
    mul x2, local copies, waits for them, and re-layouts, per_device(): inputs = [places * rows, weights, coefs[:, :, start:start + rows]]  1.62 us
  transfers between devices with their start and end apart: 9, of which 4 were waited for; matrix products, arithmetic and copies ran while one was open for 4% of the time, Pallas kernels for 35%

profile of v4, /device:TPU:0, one launch (start us, length us, event | category | flops | bytes accessed | tf_op | source)
XLA Modules:
  0.0 67.5 jit_solution(1712845182934687802)
XLA Ops:
  0.0 1.5 %copy-done.1 = f32[112,4096]{1,0:T(8,128)S(1)} copy-done((f32[112,4096]{1,0:T(8,128)S(1)}, f32[112,4096]{1,0:T(8,128)}, u32[]{:S(2)}) %copy-start.1) | copy-done | bytes 1835032
  1.5 0.5 shard_map.73
  2.1 3.0 %collective-permute-start.1 = (f32[1792,128]{1,0:T(8,128)S(1)}, f32[1792,128]{1,0:T(8,128)}, u32[]{:S(2)}, u32[]{:S(2)}) collective-permute-start(f32[1792,128]{1,0:T(8,128)S(1)} %get-tuple-element.18.refs_3_), channel_id=1, source_target_pairs={{2,0},{3,1},{0,2},{1,3},{6,4},{7,5},{4,6},{5,7},{10,8},{11,9},{8,1... | collective-permute-start | bytes 2752520 | tf_op jit(solution)/shard_map/ppermute | solution.py:287
  5.1 9.3 %shard_map.74 = (f32[112,512]{1,0:T(8,128)S(1)}, f32[4,16,128]{2,1,0:T(8,128)S(1)}) custom-call(s32[1,512]{1,0:T(1,128)S(1)} %bitcast.23, f32[112,4096]{1,0:T(8,128)S(1)} %copy-done.1, f32[13,4096]{1,0:T(8,128)S(1)} %copy-done), custom_call_target="tpu_custom_call" | custom-call | flops 8000000000 | bytes 2097152 | tf_op jit(solution)/shard_map/pallas_call | solution.py:328
  14.5 0.1 collective-permute-start.5
  14.6 0.5 collective-permute-start
  15.1 0.1 add_multiply_fusion
  15.2 0.7 %copy.9 = s32[24,112]{0,1:T(8,128)} copy(s32[24,112]{1,0:T(8,128)S(1)} %bitcast.28) | data formatting | bytes 21504 | tf_op jit(solution)/shard_map/mul | solution.py:391
  15.9 0.9 %mul.69.refs_0_ = s32[2688]{0:T(1024)S(1)} reshape(s32[112,24]{1,0:T(8,128)} %bitcast.26) | data formatting | bytes 21504 | tf_op jit(solution)/shard_map/mul | solution.py:391
  17.5 0.1 fusion.9
  17.7 0.1 copy.10
  17.8 0.1 reshape.60.refs_1_
  17.9 0.1 fusion.3
  17.9 0.1 fusion
  18.1 7.5 %collective-permute-done.1.refs_5_ = f32[1792,128]{1,0:T(8,128)} collective-permute-done((f32[1792,128]{1,0:T(8,128)S(1)}, f32[1792,128]{1,0:T(8,128)}, u32[]{:S(2)}, u32[]{:S(2)}) %collective-permute-start.1) | collective-permute-done | bytes 917536 | tf_op jit(solution)/shard_map/ppermute | solution.py:287
  25.6 1.8 %collective-permute-start.6 = (f32[112,512]{1,0:T(8,128)S(1)}, f32[112,512]{1,0:T(8,128)S(1)}, u32[]{:S(2)}, u32[]{:S(2)}) collective-permute-start(f32[112,512]{1,0:T(8,128)S(1)} %get-tuple-element.23.refs_8_), channel_id=1, source_target_pairs={{2,0},{3,1},{0,2},{1,3},{6,4},{7,5},{4,6},{5,7},{10,8},{11,9},{8,1... | collective-permute-start | bytes 688136 | tf_op jit(solution)/shard_map/ppermute | solution.py:287
  27.4 0.1 pad_bitcast_fusion.1
  27.6 6.1 %collective-permute-done.6.refs_10_ = f32[112,512]{1,0:T(8,128)S(1)} collective-permute-done((f32[112,512]{1,0:T(8,128)S(1)}, f32[112,512]{1,0:T(8,128)S(1)}, u32[]{:S(2)}, u32[]{:S(2)}) %collective-permute-start.6) | collective-permute-done | bytes 229408 | tf_op jit(solution)/shard_map/ppermute | solution.py:287
  33.8 1.8 %collective-permute-start.2 = (f32[1792,128]{1,0:T(8,128)S(1)}, f32[1792,128]{1,0:T(8,128)S(1)}, u32[]{:S(2)}, u32[]{:S(2)}) collective-permute-start(f32[1792,128]{1,0:T(8,128)S(1)} %get-tuple-element.21.refs_3_), channel_id=1, source_target_pairs={{2,0},{3,1},{0,2},{1,3},{6,4},{7,5},{4,6},{5,7},{10,8},{11,9},{8,1... | collective-permute-start | bytes 2752520 | tf_op jit(solution)/shard_map/ppermute | solution.py:287
  35.6 9.8 %shard_map.75 = (f32[112,2048]{1,0:T(8,128)S(1)}, f32[112,128]{1,0:T(8,128)S(1)}, f32[112,128]{1,0:T(8,128)S(1)}, f32[112,512]{1,0:T(8,128)S(1)}) custom-call(s32[2688]{0:T(1024)S(1)} %mul.69.refs_0_, f32[2688]{0:T(1024)S(1)} %reshape.60.refs_1_, f32[4,13,16,128]{3,2,1,0:T(8,128)S(1)} %get-tuple-element.29.refs_2_, ...), custom_call_target="tpu_custom_call" | custom-call | flops 6000000000 | bytes 3670016 | tf_op jit(solution)/shard_map/pallas_call | solution.py:417
  45.4 4.2 %shard_map.76.refs_10_ = f32[112,4096]{1,0:T(8,128)S(1)} custom-call(s32[1,512]{1,0:T(1,128)S(1)} %bitcast.24, f32[112,512]{1,0:T(8,128)S(1)} %get-tuple-element.24.flux_ref), custom_call_target="tpu_custom_call" | custom-call | flops 4000000000 | bytes 1835008 | tf_op jit(solution)/shard_map/pallas_call | solution.py:442
  49.6 7.0 %collective-permute-done.2.refs_5_ = f32[1792,128]{1,0:T(8,128)S(1)} collective-permute-done((f32[1792,128]{1,0:T(8,128)S(1)}, f32[1792,128]{1,0:T(8,128)S(1)}, u32[]{:S(2)}, u32[]{:S(2)}) %collective-permute-start.2) | collective-permute-done | bytes 917536 | tf_op jit(solution)/shard_map/ppermute | solution.py:287
  56.6 2.4 %collective-permute-done.8.refs_6_ = f32[1792,128]{1,0:T(8,128)S(1)} collective-permute-done((f32[1792,128]{1,0:T(8,128)S(1)}, f32[1792,128]{1,0:T(8,128)S(1)}, u32[]{:S(2)}, u32[]{:S(2)}) %collective-permute-start.8) | collective-permute-done | bytes 917536 | tf_op jit(solution)/shard_map/ppermute | solution.py:297
  59.1 8.5 %shard_map.77 = f32[112,4096]{1,0:T(8,128)} custom-call(s32[2688]{0:T(1024)S(1)} %mul.69.refs_0_, f32[2688]{0:T(1024)S(1)} %reshape.60.refs_1_, f32[4,13,16,128]{3,2,1,0:T(8,128)S(1)} %get-tuple-element.30.refs_2_, f32[1792,128]{1,0:T(8,128)S(1)} %get-tuple-element.21.refs_3_, f32[1792,128]{1,0:T(8,128)S(1)} %collective-permute-done.refs_4_, ...), custom_call_target="tpu_custom_call" | custom-call | flops 6000000000 | bytes 3670016 | tf_op jit(solution)/shard_map/pallas_call | solution.py:417
  (30 shorter events, 0.3 us)
Async XLA Ops:
  0.0 5.1 %copy-start = (f32[13,4096]{1,0:T(8,128)S(1)}, f32[13,4096]{1,0:T(8,128)}, u32[]{:S(2)}) copy-start(f32[13,4096]{1,0:T(8,128)} %kl_ref.1) | copy-start | bytes 638980
  0.0 1.5 %copy-start.1 = (f32[112,4096]{1,0:T(8,128)S(1)}, f32[112,4096]{1,0:T(8,128)}, u32[]{:S(2)}) copy-start(f32[112,4096]{1,0:T(8,128)} %field_ref.3) | copy-start | bytes 5505028
  1.5 3.6 %copy-start.2 = (s32[1,4,128]{2,1,0:T(4,128)S(1)}, s32[1,4,128]{2,1,0:T(4,128)}, u32[]{:S(2)}) copy-start(s32[1,4,128]{2,1,0:T(4,128)} %param.13) | copy-start | bytes 6148
  2.1 23.5 %collective-permute-start.1 = (f32[1792,128]{1,0:T(8,128)S(1)}, f32[1792,128]{1,0:T(8,128)}, u32[]{:S(2)}, u32[]{:S(2)}) collective-permute-start(f32[1792,128]{1,0:T(8,128)S(1)} %get-tuple-element.18.refs_3_), channel_id=1, source_target_pairs={{2,0},{3,1},{0,2},{1,3},{6,4},{7,5},{4,6},{5,7},{10,8},{11,9},{8,1... | collective-permute-start | bytes 2752520 | tf_op jit(solution)/shard_map/ppermute | solution.py:287
  5.1 30.5 %collective-permute-start.3 = (f32[1792,128]{1,0:T(8,128)S(1)}, f32[1792,128]{1,0:T(8,128)}, u32[]{:S(2)}, u32[]{:S(2)}) collective-permute-start(f32[1792,128]{1,0:T(8,128)S(1)} %get-tuple-element.18.refs_3_), channel_id=1, source_target_pairs={{0,1},{1,0},{2,3},{3,2},{4,5},{5,4},{6,7},{7,6},{8,9},{9,8},{10,11... | collective-permute-start | bytes 2752520 | tf_op jit(solution)/shard_map/ppermute | solution.py:297
  5.1 10.0 %copy-start.3 = (s32[12,2,112]{2,1,0:T(2,128)S(1)}, s32[12,2,112]{2,1,0:T(2,128)}, u32[]{:S(2)}) copy-start(s32[12,2,112]{2,1,0:T(2,128)} %param.9) | copy-start | bytes 32260
  5.1 12.4 %copy-start.5 = (s32[1,4]{1,0:T(1,128)S(1)}, s32[1,4]{1,0:T(1,128)}, u32[]{:S(2)}) copy-start(s32[1,4]{1,0:T(1,128)} %param.12) | copy-start | bytes 52
  5.1 12.5 %copy-start.4 = (f32[12,2,112]{2,1,0:T(2,128)S(1)}, f32[12,2,112]{2,1,0:T(2,128)}, u32[]{:S(2)}) copy-start(f32[12,2,112]{2,1,0:T(2,128)} %param.10) | copy-start | bytes 32260
  14.5 19.3 %collective-permute-start.5 = (f32[112,512]{1,0:T(8,128)S(1)}, f32[112,512]{1,0:T(8,128)S(1)}, u32[]{:S(2)}, u32[]{:S(2)}) collective-permute-start(f32[112,512]{1,0:T(8,128)S(1)} %get-tuple-element.23.refs_8_), channel_id=1, source_target_pairs={{0,1},{1,0},{2,3},{3,2},{4,5},{5,4},{6,7},{7,6},{8,9},{9,8},{10,11... | collective-permute-start | bytes 688136 | tf_op jit(solution)/shard_map/ppermute | solution.py:297
  14.6 42.0 %collective-permute-start = (f32[1792,128]{1,0:T(8,128)S(1)}, f32[1792,128]{1,0:T(8,128)S(1)}, u32[]{:S(2)}, u32[]{:S(2)}) collective-permute-start(f32[1792,128]{1,0:T(8,128)S(1)} %get-tuple-element.21.refs_3_), channel_id=1, source_target_pairs={{0,1},{1,0},{2,3},{3,2},{4,5},{5,4},{6,7},{7,6},{8,9},{9,8},{10,11... | collective-permute-start | bytes 2752520 | tf_op jit(solution)/shard_map/ppermute | solution.py:297
  25.6 10.0 %collective-permute-start.4 = (f32[1792,128]{1,0:T(8,128)}, f32[1792,128]{1,0:T(8,128)S(1)}, u32[]{:S(2)}, u32[]{:S(2)}) collective-permute-start(f32[1792,128]{1,0:T(8,128)} %collective-permute-done.1.refs_5_), channel_id=1, source_target_pairs={{0,1},{1,0},{2,3},{3,2},{4,5},{5,4},{6,7},{7,6},{8,9},{9,8},{10,11... | collective-permute-start | bytes 2752520 | tf_op jit(solution)/shard_map/ppermute | solution.py:297
  25.6 8.1 %collective-permute-start.6 = (f32[112,512]{1,0:T(8,128)S(1)}, f32[112,512]{1,0:T(8,128)S(1)}, u32[]{:S(2)}, u32[]{:S(2)}) collective-permute-start(f32[112,512]{1,0:T(8,128)S(1)} %get-tuple-element.23.refs_8_), channel_id=1, source_target_pairs={{2,0},{3,1},{0,2},{1,3},{6,4},{7,5},{4,6},{5,7},{10,8},{11,9},{8,1... | collective-permute-start | bytes 688136 | tf_op jit(solution)/shard_map/ppermute | solution.py:287
  33.7 1.9 %collective-permute-start.7 = (f32[112,512]{1,0:T(8,128)S(1)}, f32[112,512]{1,0:T(8,128)S(1)}, u32[]{:S(2)}, u32[]{:S(2)}) collective-permute-start(f32[112,512]{1,0:T(8,128)S(1)} %collective-permute-done.6.refs_10_), channel_id=1, source_target_pairs={{0,1},{1,0},{2,3},{3,2},{4,5},{5,4},{6,7},{7,6},{8,9},{9,8},{10,11... | collective-permute-start | bytes 688136 | tf_op jit(solution)/shard_map/ppermute | solution.py:297
  33.8 22.8 %collective-permute-start.2 = (f32[1792,128]{1,0:T(8,128)S(1)}, f32[1792,128]{1,0:T(8,128)S(1)}, u32[]{:S(2)}, u32[]{:S(2)}) collective-permute-start(f32[1792,128]{1,0:T(8,128)S(1)} %get-tuple-element.21.refs_3_), channel_id=1, source_target_pairs={{2,0},{3,1},{0,2},{1,3},{6,4},{7,5},{4,6},{5,7},{10,8},{11,9},{8,1... | collective-permute-start | bytes 2752520 | tf_op jit(solution)/shard_map/ppermute | solution.py:287
  56.6 2.5 %collective-permute-start.8 = (f32[1792,128]{1,0:T(8,128)S(1)}, f32[1792,128]{1,0:T(8,128)S(1)}, u32[]{:S(2)}, u32[]{:S(2)}) collective-permute-start(f32[1792,128]{1,0:T(8,128)S(1)} %collective-permute-done.2.refs_5_), channel_id=1, source_target_pairs={{0,1},{1,0},{2,3},{3,2},{4,5},{5,4},{6,7},{7,6},{8,9},{9,8},{10,11... | collective-permute-start | bytes 2752520 | tf_op jit(solution)/shard_map/ppermute | solution.py:297
